TPU v7x, 32 devices: a whole 2x2x4 slice. The times are simulated.
32 devices in a mesh: groups: 2 (over y), gx: 4 (over z), gy: 4 (over x, core).
Axes of the slice: x: 2, y: 2, z: 4, core: 2. Of those that a mesh axis runs over, the one named last changes fastest.
Arguments:
- latent: bfloat16 [32, 32, 8, 256], P(('groups', 'gx'), 'gy'), parts along dimension 0, may hold values from -6 to 6
- positions: bfloat16 [32, 32, 8, 2], P(('groups', 'gx'), 'gy'), parts along dimension 0, may hold values from 0 to 1
- counts: int32 [32, 32], P(('groups', 'gx'), 'gy'), parts along dimension 0, may hold values from 1 to 8, as said below
- cotangent: bfloat16 [32, 32, 8, 256], P(('groups', 'gx'), 'gy'), parts along dimension 0, may hold values from -6 to 6
- w_recv: bfloat16 [256, 256], replicated, may hold values from -0.375 to 0.375
- w_send: bfloat16 [256, 256], replicated, may hold values from -0.375 to 0.375
- w_msg: bfloat16 [256, 256], replicated, may hold values from -0.375 to 0.375
- w_node_h: bfloat16 [256, 256], replicated, may hold values from -0.375 to 0.375
- w_node_m: bfloat16 [256, 256], replicated, may hold values from -0.375 to 0.375
- w_out: bfloat16 [256, 256], replicated, may hold values from -0.375 to 0.375
- geometry: float32 [3, 256], replicated, may hold values from -3 to 3
- gain: float32 [256], replicated, may hold values from 0.5 to 1.5
Outputs:
- latent_out: bfloat16 [32, 32, 8, 256], P(('groups', 'gx'), 'gy'), parts along dimension 0
- grad_latent: bfloat16 [32, 32, 8, 256], P(('groups', 'gx'), 'gy'), parts along dimension 0
- grad_recv: float32 [512, 256], P('groups'), parts along dimension 0
- grad_send: float32 [512, 256], P('groups'), parts along dimension 0
- grad_msg: float32 [512, 256], P('groups'), parts along dimension 0
- grad_node_h: float32 [512, 256], P('groups'), parts along dimension 0
- grad_node_m: float32 [512, 256], P('groups'), parts along dimension 0
- grad_out: float32 [512, 256], P('groups'), parts along dimension 0
- grad_geometry: float32 [6, 256], P('groups'), parts along dimension 0
- grad_gain: float32 [512], P('groups'), parts along dimension 0
There are 2 independent parts, one for each index of `groups`. A program takes and returns all parts, laid end to end along the dimension named above; an argument that names none is the same for every part. Nothing has to cross between parts.
Inputs may be any that keep to these rules, and one draw needn't show every extreme that they name: `counts`: slots below a cell's count hold particles, the others are padding; some cell holds 8 particles in every draw, and whole blocks of 4 x 8 cells are one to four times denser than others.
All inputs are finite; a program needn't handle non-finite values.
Results may differ from a plain program's by a relative error of at most 0.019.
The roundings to bfloat16 on the way count: a program that leaves them out, or rounds other values in their place, can miss the bound.
Values may be sent and summed in bfloat16 or wider, within the bound.
A program may use at most 64 MiB of HBM per device.

v0:
```python
from functools import partial

import jax
import jax.numpy as jnp
from jax import lax
from jax.sharding import PartitionSpec as P

STEPS = 2


EPSILON = 1e-05
OFFSETS = ((-1, -1), (-1, 0), (-1, 1), (0, -1), (0, 0), (0, 1), (1, -1), (1, 0), (1, 1))


def for_sending(array):

    def short(part):
        return part.astype(jnp.bfloat16) if part.dtype == jnp.float32 else part

    return jax.tree.map(short, array)


def passed_along(block, axis, distance):
    devices = range(lax.axis_size(axis))
    route = [((i - distance) % len(devices), i) for i in devices]
    return lax.ppermute(block, axis, route)


def extended(cells, sides, width):
    for axis, dim in sides:
        count = lax.axis_size(axis)
        head = lax.slice_in_dim(cells, 0, width, axis=dim)
        tail = lax.slice_in_dim(cells, cells.shape[dim] - width, cells.shape[dim], axis=dim)
        cells = jnp.concatenate(
            [
                lax.ppermute(tail, axis, [(i, (i + 1) % count) for i in range(count)]),
                cells,
                lax.ppermute(head, axis, [((i + 1) % count, i) for i in range(count)]),
            ],
            axis=dim,
        )
    return cells


def pair_row(shift_x, shift_y, geometry, pieces):
    recv_proj, send_proj, recv_pos, send_pos, recv_valid, send_valid = pieces
    disp_x = send_pos[..., None, :, 0] + shift_x - recv_pos[..., :, None, 0]
    disp_y = send_pos[..., None, :, 1] + shift_y - recv_pos[..., :, None, 1]
    dist_sq = disp_x * disp_x + disp_y * disp_y
    pair_weight = recv_valid[..., :, None] * send_valid[..., None, :] / (1.0 + dist_sq)
    if shift_x == 0 and shift_y == 0:
        slots = recv_proj.shape[-2]
        pair_weight = pair_weight * (1.0 - jnp.eye(slots, dtype=jnp.float32))
    preact = (
        recv_proj[..., :, None, :]
        + send_proj[..., None, :, :]
        + disp_x[..., None] * geometry[0]
        + disp_y[..., None] * geometry[1]
        + dist_sq[..., None] * geometry[2]
    )
    return jnp.sum(pair_weight[..., None] * jax.nn.silu(preact), axis=-2)


def offset_terms(shift_x, shift_y, geometry, pieces):
    cell_fn = jax.checkpoint(partial(pair_row, shift_x, shift_y, geometry))
    return cell_fn(pieces)


def layer_norm(values, gain):
    center = values - jnp.mean(values, axis=-1, keepdims=True)
    spread = jnp.mean(center * center, axis=-1, keepdims=True)
    return center * lax.rsqrt(spread + EPSILON) * gain


def send_part(w_send, latent32, tap_send):
    product = jnp.dot(latent32.astype(jnp.bfloat16), w_send, preferred_element_type=jnp.float32)
    return (product + tap_send).astype(jnp.bfloat16)


def receive_part(
    weights,
    local_pos,
    local_valid,
    edge_pos,
    edge_valid,
    latent32,
    send_ext,
    tap_recv,
    tap_msg,
    tap_pre,
    tap_out,
    geometry,
    gain,
):
    w_recv, w_msg, w_node_h, w_node_m, w_out = weights
    cells_x, cells_y = (latent32.shape[0], latent32.shape[1])
    latent16 = latent32.astype(jnp.bfloat16)
    recv_proj = jnp.dot(latent16, w_recv, preferred_element_type=jnp.float32) + tap_recv
    total = jnp.zeros(recv_proj.shape, jnp.float32)
    for shift_x, shift_y in OFFSETS:
        low_x, low_y = (1 + shift_x, 1 + shift_y)
        send_proj = send_ext[low_x : low_x + cells_x, low_y : low_y + cells_y]
        send_pos = edge_pos[low_x : low_x + cells_x, low_y : low_y + cells_y]
        send_valid = edge_valid[low_x : low_x + cells_x, low_y : low_y + cells_y]
        total = total + offset_terms(
            shift_x,
            shift_y,
            geometry,
            (recv_proj, send_proj, local_pos, send_pos, local_valid, send_valid),
        )
    aggregate = total.astype(jnp.bfloat16)
    message = (jnp.dot(aggregate, w_msg, preferred_element_type=jnp.float32) + tap_msg).astype(
        jnp.bfloat16
    )
    hidden = (
        jnp.dot(latent16, w_node_h, preferred_element_type=jnp.float32)
        + jnp.dot(message, w_node_m, preferred_element_type=jnp.float32)
        + tap_pre
    )
    active = jax.nn.silu(hidden).astype(jnp.bfloat16)
    output = jnp.dot(active, w_out, preferred_element_type=jnp.float32) + tap_out
    updated = (latent32 + layer_norm(output, gain)).astype(jnp.bfloat16)
    return (updated, (latent16, aggregate, message, active))


def outer_sum(inputs16, derivs):
    width = derivs.shape[-1]
    return lax.dot_general(
        inputs16.reshape(-1, inputs16.shape[-1]).astype(jnp.float32),
        derivs.reshape(-1, width),
        (((0,), (0,)), ((), ())),
        precision=lax.Precision.HIGHEST,
    )


def return_rim(ext_grad):
    inner = ext_grad[:, 1:-1]
    for shift_by, edge_index in ((-1, 0), (1, -1)):
        arrived = passed_along(for_sending(ext_grad[:, edge_index]), "gy", shift_by)
        target = -1 if shift_by == -1 else 0
        inner = inner.at[:, target].add(arrived)
    core = inner[1:-1]
    for shift_by, edge_index in ((-1, 0), (1, -1)):
        arrived = passed_along(for_sending(inner[edge_index]), "gx", shift_by)
        target = -1 if shift_by == -1 else 0
        core = core.at[target].add(arrived)
    return core


def per_device(
    latent,
    positions,
    counts,
    cotangent,
    w_recv,
    w_send,
    w_msg,
    w_node_h,
    w_node_m,
    w_out,
    geometry,
    gain,
):
    cells_x, cells_y, slots, width = latent.shape
    slot_index = lax.broadcasted_iota(jnp.int32, (cells_x, cells_y, slots), 2)
    validity16 = (slot_index < counts[:, :, None]).astype(jnp.bfloat16)
    edge_pos16, edge_valid16 = (
        extended(positions, (("gx", 0), ("gy", 1)), 1),
        extended(validity16, (("gx", 0), ("gy", 1)), 1),
    )
    local_pos = positions.astype(jnp.float32)
    local_valid = validity16.astype(jnp.float32)
    edge_pos = edge_pos16.astype(jnp.float32)
    edge_valid = edge_valid16.astype(jnp.float32)
    weights = (w_recv, w_msg, w_node_h, w_node_m, w_out)
    zeros = jnp.zeros(latent.shape, jnp.float32)
    local_fn = partial(receive_part, weights, local_pos, local_valid, edge_pos, edge_valid)
    records = []
    current = latent
    for step in range(STEPS):
        latent32 = current.astype(jnp.float32)
        send16, send_back = jax.vjp(partial(send_part, w_send), latent32, zeros)
        send_ext = extended(for_sending(send16), (("gx", 0), ("gy", 1)), 1).astype(send16.dtype)
        updated, recv_back, saved = jax.vjp(
            local_fn,
            latent32,
            send_ext.astype(jnp.float32),
            zeros,
            zeros,
            zeros,
            zeros,
            geometry,
            gain,
            has_aux=True,
        )
        records.append((send_back, recv_back, saved))
        current = updated
    flow = cotangent
    totals = tuple(
        (
            jnp.zeros(shape_item, jnp.float32)
            for shape_item in [(width, width)] * 6 + [geometry.shape, gain.shape]
        )
    )
    for send_back, recv_back, saved in reversed(records):
        g_latent, g_send_ext, g_recv, g_msg, g_pre, g_out, g_geom, g_gain = recv_back(flow)
        g_send32 = return_rim(g_send_ext)
        g_latent_b, g_tap_send = send_back(g_send32.astype(jnp.bfloat16))
        latent16, aggregate, message, active = saved
        step_terms = (
            outer_sum(latent16, g_recv),
            outer_sum(latent16, g_tap_send),
            outer_sum(aggregate, g_msg),
            outer_sum(latent16, g_pre),
            outer_sum(message, g_pre),
            outer_sum(active, g_out),
            g_geom,
            g_gain,
        )
        totals = tuple(
            (total_item + term_item for total_item, term_item in zip(totals, step_terms))
        )
        flow = (g_latent + g_latent_b).astype(jnp.bfloat16)
    totals = lax.psum(totals, ("gx", "gy"))
    return (current, flow) + tuple(totals)


def solution(mesh):
    placed = (
        P(("groups", "gx"), "gy", None, None),
        P(("groups", "gx"), "gy", None, None),
        P(("groups", "gx"), "gy"),
        P(("groups", "gx"), "gy", None, None),
        P(),
        P(),
        P(),
        P(),
        P(),
        P(),
        P(),
        P(),
    )
    return jax.shard_map(
        per_device,
        mesh=mesh,
        in_specs=placed,
        out_specs=(
            P(("groups", "gx"), "gy", None, None),
            P(("groups", "gx"), "gy", None, None),
            P("groups", None),
            P("groups", None),
            P("groups", None),
            P("groups", None),
            P("groups", None),
            P("groups", None),
            P("groups", None),
            P("groups"),
        ),
        check_vma=False,
    )
```

profile of v0, /device:TPU:0, one launch (start us, length us, event | category | flops | bytes accessed | tf_op | source)
XLA Modules:
  0.0 277.2 jit_solution(17217789822892068159)
XLA Ops:
  7.3 0.9 fusion.124
  8.1 3.0 %collective-permute-start = (bf16[1,8,8]{2,1,0:T(8,128)(2,1)S(1)}, bf16[1,8,8]{2,1,0:T(8,128)(2,1)S(1)}, u32[]{:S(2)}, u32[]{:S(2)}) collective-permute-start(bf16[1,8,8]{2,1,0:T(8,128)(2,1)S(1)} %get-tuple-element.799), channel_id=1, source_target_pairs={{0,4},{4,8},{8,12},{12,0},{1,5},{5,9},{9,13},{13,1},{2,6},{6,10},{... | collective-permute-start | bytes 392 | tf_op jit(solution)/shard_map/ppermute | solution.py:36
  11.2 2.1 collective-permute-start.1
  13.2 0.7 fusion.199
  14.0 3.8 %collective-permute-start.5 = (bf16[1,8,8,2]{2,3,1,0:T(2,128)(2,1)S(1)}, bf16[1,8,8,2]{2,3,1,0:T(2,128)(2,1)S(1)}, u32[]{:S(2)}, u32[]{:S(2)}) collective-permute-start(bf16[1,8,8,2]{2,3,1,0:T(2,128)(2,1)S(1)} %get-tuple-element.795), channel_id=1, source_target_pairs={{4,0},{8,4},{12,8},{0,12},{5,1},{9,5},{13,9},{1,13},{6,2},{10,6},{... | collective-permute-start | bytes 776 | tf_op jit(solution)/shard_map/ppermute | solution.py:38
  17.8 1.1 convolution_convert_fusion.15
  19.7 1.7 collective-permute-start.3
  21.4 1.3 collective-permute-done.2
  22.7 3.8 %collective-permute-start.9 = (bf16[1,8,8,256]{3,2,1,0:T(8,128)(2,1)S(1)}, bf16[1,8,8,256]{3,2,1,0:T(8,128)(2,1)S(1)}, u32[]{:S(2)}, u32[]{:S(2)}) collective-permute-start(bf16[1,8,8,256]{3,2,1,0:T(8,128)(2,1)S(1)} %get-tuple-element.556), channel_id=1, source_target_pairs={{4,0},{8,4},{12,8},{0,12},{5,1},{9,5},{13,9},{1,13},{6,2},{10,6},{... | collective-permute-start | bytes 98312 | tf_op jit(solution)/shard_map/ppermute | solution.py:38
  26.7 1.7 collective-permute-start.7
  28.4 1.3 collective-permute-done.6
  30.7 1.8 collective-permute-start.10
  32.6 1.4 collective-permute-done.10
  34.3 5.0 %multiply_reduce_fusion.70 = (f32[4,8,8,256]{3,2,1,0:T(8,128)S(1)}, f32[4,8,8,256]{3,2,1,0:T(8,128)S(1)}, f32[4,8,8,256]{3,2,1,0:T(8,128)S(1)}) fusion(f32[4,8,8,8]{3,2,1,0:T(8,128)S(1)} %get-tuple-element.657, f32[4,8,8,8]{3,2,1,0:T(8,128)S(1)} %get-tuple-element.664, f32[4,8,8,8]{3,2,1,0:T(8,128)S(1)} %get-tuple-element.661, ...), kind=kLoop, calls=%fused_computation.214 | loop fusion | flops 20250624 | bytes 1936384 | tf_op jit(solution)/shard_map/jvp()/reduce_sum | solution.py:61
  39.3 5.0 %multiply_reduce_fusion.71 = (f32[4,8,8,256]{3,2,1,0:T(8,128)S(1)}, f32[4,8,8,256]{3,2,1,0:T(8,128)S(1)}, f32[4,8,8,256]{3,2,1,0:T(8,128)S(1)}) fusion(f32[256]{0:T(256)S(1)} %bitcast.544, f32[4,8,8,8]{3,2,1,0:T(8,128)S(1)} %get-tuple-element.659, f32[256]{0:T(256)S(1)} %bitcast.550, f32[4,8,8,8]{3,2,1,0:T(8,128)S(1)} %get-tuple-element.666, ...), kind=kLoop, calls=%fused_computation.215 | loop fusion | flops 20250624 | bytes 1936384 | tf_op jit(solution)/shard_map/jvp()/reduce_sum | solution.py:61
  44.2 5.0 %multiply_reduce_fusion.65 = (f32[4,8,8,256]{3,2,1,0:T(8,128)S(1)}, f32[4,8,8,256]{3,2,1,0:T(8,128)S(1)}, f32[4,8,8,256]{3,2,1,0:T(8,128)S(1)}) fusion(f32[4,8,8,8]{3,2,1,0:T(8,128)S(1)} %get-tuple-element.642, f32[4,8,8,8]{3,2,1,0:T(8,128)S(1)} %get-tuple-element.672, f32[4,8,8,8]{3,2,1,0:T(8,128)S(1)} %get-tuple-element.668, ...), kind=kLoop, calls=%fused_computation.209 | loop fusion | flops 20250624 | bytes 1936384 | tf_op jit(solution)/shard_map/jvp()/reduce_sum | solution.py:61
  49.4 0.7 copy-done.3
  52.0 3.8 %collective-permute-start.13 = (bf16[1,8,8,256]{3,2,1,0:T(8,128)(2,1)S(1)}, bf16[1,8,8,256]{3,2,1,0:T(8,128)(2,1)S(1)}, u32[]{:S(2)}, u32[]{:S(2)}) collective-permute-start(bf16[1,8,8,256]{3,2,1,0:T(8,128)(2,1)S(1)} %get-tuple-element.554), channel_id=1, source_target_pairs={{4,0},{8,4},{12,8},{0,12},{5,1},{9,5},{13,9},{1,13},{6,2},{10,6},{... | collective-permute-start | bytes 98312 | tf_op jit(solution)/shard_map/ppermute | solution.py:38
  56.0 1.7 collective-permute-done.12
  58.4 1.1 collective-permute-start.15
  59.7 1.3 collective-permute-done.14
  61.3 5.1 %multiply_reduce_fusion.61 = (f32[4,8,8,256]{3,2,1,0:T(8,128)S(1)}, f32[4,8,8,256]{3,2,1,0:T(8,128)S(1)}, f32[4,8,8,256]{3,2,1,0:T(8,128)S(1)}) fusion(f32[4,8,8,256]{3,2,1,0:T(8,128)S(1)} %get-tuple-element.312, f32[4,8,8,256]{3,2,1,0:T(8,128)S(1)} %fusion.91, f32[4,8,8,8]{3,2,1,0:T(8,128)S(1)} %get-tuple-element.657, ...), kind=kLoop, calls=%fused_computation.205 | loop fusion | flops 20250624 | bytes 1936384 | tf_op jit(solution)/shard_map/jvp()/reduce_sum | solution.py:61
  66.4 4.9 %multiply_reduce_fusion.62 = (f32[4,8,8,256]{3,2,1,0:T(8,128)S(1)}, f32[4,8,8,256]{3,2,1,0:T(8,128)S(1)}, f32[4,8,8,256]{3,2,1,0:T(8,128)S(1)}) fusion(f32[4,8,8,256]{3,2,1,0:T(8,128)S(1)} %get-tuple-element.320, f32[4,8,8,256]{3,2,1,0:T(8,128)S(1)} %fusion.91, f32[256]{0:T(256)S(1)} %bitcast.547, f32[4,8,8,8]{3,2,1,0:T(8,128)S(1)} %get-tuple-element.659, ...), kind=kLoop, calls=%fused_computation.206 | loop fusion | flops 20250624 | bytes 1936384 | tf_op jit(solution)/shard_map/jvp()/reduce_sum | solution.py:61
  71.4 5.0 %multiply_reduce_fusion.56 = (f32[4,8,8,256]{3,2,1,0:T(8,128)S(1)}, f32[4,8,8,256]{3,2,1,0:T(8,128)S(1)}, f32[4,8,8,256]{3,2,1,0:T(8,128)S(1)}) fusion(f32[4,8,8,256]{3,2,1,0:T(8,128)S(1)} %get-tuple-element.272, f32[4,8,8,256]{3,2,1,0:T(8,128)S(1)} %fusion.91, f32[4,8,8,8]{3,2,1,0:T(8,128)S(1)} %get-tuple-element.642, ...), kind=kLoop, calls=%fused_computation.200 | loop fusion | flops 20250624 | bytes 1936384 | tf_op jit(solution)/shard_map/jvp()/reduce_sum | solution.py:61
  78.1 0.9 fusion.62
  82.0 2.8 %multiply_reduce_fusion.50 = (f32[256]{0:T(256)S(1)}, f32[4,8,8,256]{3,2,1,0:T(8,128)S(1)}, f32[256]{0:T(256)S(1)}, f32[256]{0:T(256)S(1)}, f32[4,8,8,256]{3,2,1,0:T(8,128)S(1)}) fusion(f32[4,8,8,8]{3,2,1,0:T(8,128)S(1)} %get-tuple-element.576, f32[256]{0:T(256)S(1)} %bitcast.607, f32[256]{0:T(256)S(1)} %bitcast.608, ...), kind=kLoop, calls=%fused_computation.194 | loop fusion | flops 12975360 | bytes 1349632 | tf_op jit(solution)/shard_map/transpose(jvp(jvp()))/checkpoint/reduce_sum | solution.py:59
  84.8 2.8 %multiply_reduce_fusion.53 = (f32[256]{0:T(256)S(1)}, f32[4,8,8,256]{3,2,1,0:T(8,128)S(1)}, f32[256]{0:T(256)S(1)}, f32[256]{0:T(256)S(1)}, f32[4,8,8,256]{3,2,1,0:T(8,128)S(1)}) fusion(f32[4,8,8,8]{3,2,1,0:T(8,128)S(1)} %get-tuple-element.578, f32[256]{0:T(256)S(1)} %bitcast.604, f32[256]{0:T(256)S(1)} %bitcast.605, ...), kind=kLoop, calls=%fused_computation.197 | loop fusion | flops 12975360 | bytes 1349632 | tf_op jit(solution)/shard_map/transpose(jvp(jvp()))/checkpoint/reduce_sum | solution.py:59
  87.6 2.8 %multiply_reduce_fusion.47 = (f32[256]{0:T(256)S(1)}, f32[4,8,8,256]{3,2,1,0:T(8,128)S(1)}, f32[256]{0:T(256)S(1)}, f32[256]{0:T(256)S(1)}, f32[4,8,8,256]{3,2,1,0:T(8,128)S(1)}) fusion(f32[4,8,8,8]{3,2,1,0:T(8,128)S(1)} %get-tuple-element.580, f32[256]{0:T(256)S(1)} %bitcast.601, f32[256]{0:T(256)S(1)} %bitcast.602, ...), kind=kLoop, calls=%fused_computation.191 | loop fusion | flops 12975360 | bytes 1349632 | tf_op jit(solution)/shard_map/transpose(jvp(jvp()))/checkpoint/reduce_sum | solution.py:59
  90.4 2.8 %multiply_reduce_fusion.44 = (f32[256]{0:T(256)S(1)}, f32[4,8,8,256]{3,2,1,0:T(8,128)S(1)}, f32[256]{0:T(256)S(1)}, f32[256]{0:T(256)S(1)}, f32[4,8,8,256]{3,2,1,0:T(8,128)S(1)}) fusion(f32[4,8,8,8]{3,2,1,0:T(8,128)S(1)} %get-tuple-element.582, f32[256]{0:T(256)S(1)} %bitcast.598, f32[256]{0:T(256)S(1)} %bitcast.599, ...), kind=kLoop, calls=%fused_computation.188 | loop fusion | flops 12975360 | bytes 1349632 | tf_op jit(solution)/shard_map/transpose(jvp(jvp()))/checkpoint/reduce_sum | solution.py:59
  93.2 2.8 %multiply_reduce_fusion.41 = (f32[256]{0:T(256)S(1)}, f32[4,8,8,256]{3,2,1,0:T(8,128)S(1)}, f32[256]{0:T(256)S(1)}, f32[256]{0:T(256)S(1)}, f32[4,8,8,256]{3,2,1,0:T(8,128)S(1)}) fusion(f32[4,8,8,8]{3,2,1,0:T(8,128)S(1)} %get-tuple-element.584, f32[256]{0:T(256)S(1)} %bitcast.592, f32[256]{0:T(256)S(1)} %bitcast.593, ...), kind=kLoop, calls=%fused_computation.185 | loop fusion | flops 12975360 | bytes 1349632 | tf_op jit(solution)/shard_map/transpose(jvp(jvp()))/checkpoint/reduce_sum | solution.py:59
  96.0 2.8 %multiply_reduce_fusion.38 = (f32[256]{0:T(256)S(1)}, f32[4,8,8,256]{3,2,1,0:T(8,128)S(1)}, f32[256]{0:T(256)S(1)}, f32[256]{0:T(256)S(1)}, f32[4,8,8,256]{3,2,1,0:T(8,128)S(1)}) fusion(f32[4,8,8,8]{3,2,1,0:T(8,128)S(1)} %get-tuple-element.586, f32[256]{0:T(256)S(1)} %bitcast.580, f32[256]{0:T(256)S(1)} %bitcast.581, ...), kind=kLoop, calls=%fused_computation.182 | loop fusion | flops 12975360 | bytes 1349632 | tf_op jit(solution)/shard_map/transpose(jvp(jvp()))/checkpoint/reduce_sum | solution.py:59
  98.8 2.8 %multiply_reduce_fusion.35 = (f32[256]{0:T(256)S(1)}, f32[4,8,8,256]{3,2,1,0:T(8,128)S(1)}, f32[256]{0:T(256)S(1)}, f32[256]{0:T(256)S(1)}, f32[4,8,8,256]{3,2,1,0:T(8,128)S(1)}) fusion(f32[4,8,8,8]{3,2,1,0:T(8,128)S(1)} %get-tuple-element.588, f32[256]{0:T(256)S(1)} %bitcast.571, f32[256]{0:T(256)S(1)} %bitcast.572, ...), kind=kLoop, calls=%fused_computation.179 | loop fusion | flops 12975360 | bytes 1349632 | tf_op jit(solution)/shard_map/transpose(jvp(jvp()))/checkpoint/reduce_sum | solution.py:59
  101.7 2.8 %multiply_reduce_fusion.32 = (f32[256]{0:T(256)S(1)}, f32[4,8,8,256]{3,2,1,0:T(8,128)S(1)}, f32[256]{0:T(256)S(1)}, f32[256]{0:T(256)S(1)}, f32[4,8,8,256]{3,2,1,0:T(8,128)S(1)}) fusion(f32[4,8,8,8]{3,2,1,0:T(8,128)S(1)} %get-tuple-element.590, f32[256]{0:T(256)S(1)} %bitcast.562, f32[256]{0:T(256)S(1)} %bitcast.563, ...), kind=kLoop, calls=%fused_computation.176 | loop fusion | flops 12975360 | bytes 1349632 | tf_op jit(solution)/shard_map/transpose(jvp(jvp()))/checkpoint/reduce_sum | solution.py:59
  104.5 3.0 %multiply_reduce_fusion.29 = (f32[256]{0:T(256)S(1)}, f32[4,8,8,256]{3,2,1,0:T(8,128)S(1)}, f32[256]{0:T(256)S(1)}, f32[256]{0:T(256)S(1)}, f32[4,8,8,256]{3,2,1,0:T(8,128)S(1)}) fusion(f32[4,8,8,8]{3,2,1,0:T(8,128)S(1)} %get-tuple-element.592, f32[256]{0:T(256)S(1)} %bitcast.556, f32[256]{0:T(256)S(1)} %bitcast.557, ...), kind=kLoop, calls=%fused_computation.173 | loop fusion | flops 12975360 | bytes 1349632 | tf_op jit(solution)/shard_map/transpose(jvp(jvp()))/checkpoint/reduce_sum | solution.py:59
  107.7 1.8 collective-permute-start.16
  110.3 0.8 collective-permute-done.16
  111.0 1.7 collective-permute-done.17
  112.8 3.9 %collective-permute-start.18 = (bf16[8,8,256]{2,1,0:T(8,128)(2,1)S(1)}, bf16[8,8,256]{2,1,0:T(8,128)(2,1)S(1)}, u32[]{:S(2)}, u32[]{:S(2)}) collective-permute-start(bf16[8,8,256]{2,1,0:T(8,128)(2,1)S(1)} %get-tuple-element.548), channel_id=1, source_target_pairs={{4,0},{8,4},{12,8},{0,12},{5,1},{9,5},{13,9},{1,13},{6,2},{10,6},{... | collective-permute-start | bytes 98312 | tf_op jit(solution)/shard_map/ppermute | solution.py:26
  117.1 1.2 collective-permute-done.18
  118.4 4.4 %collective-permute-done.19 = bf16[8,8,256]{2,1,0:T(8,128)(2,1)S(1)} collective-permute-done((bf16[8,8,256]{2,1,0:T(8,128)(2,1)S(1)}, bf16[8,8,256]{2,1,0:T(8,128)(2,1)S(1)}, u32[]{:S(2)}, u32[]{:S(2)}) %collective-permute-start.19) | collective-permute-done | bytes 32800 | tf_op jit(solution)/shard_map/ppermute | solution.py:26
  125.9 1.2 fusion.39
  127.1 1.0 fusion.38
  128.2 1.0 fusion.37
  130.8 2.8 %multiply_reduce_fusion.23 = (f32[256]{0:T(256)S(1)}, f32[4,8,8,256]{3,2,1,0:T(8,128)S(1)}, f32[256]{0:T(256)S(1)}, f32[256]{0:T(256)S(1)}, f32[4,8,8,256]{3,2,1,0:T(8,128)S(1)}) fusion(f32[4,8,8,8]{3,2,1,0:T(8,128)S(1)} %get-tuple-element.558, f32[256]{0:T(256)S(1)} %bitcast.595, f32[256]{0:T(256)S(1)} %bitcast.596, ...), kind=kLoop, calls=%fused_computation.167 | loop fusion | flops 12975360 | bytes 1349632 | tf_op jit(solution)/shard_map/transpose(jvp(jvp()))/checkpoint/reduce_sum | solution.py:59
  133.6 2.8 %multiply_reduce_fusion.26 = (f32[256]{0:T(256)S(1)}, f32[4,8,8,256]{3,2,1,0:T(8,128)S(1)}, f32[256]{0:T(256)S(1)}, f32[256]{0:T(256)S(1)}, f32[4,8,8,256]{3,2,1,0:T(8,128)S(1)}) fusion(f32[4,8,8,8]{3,2,1,0:T(8,128)S(1)} %get-tuple-element.560, f32[256]{0:T(256)S(1)} %bitcast.589, f32[256]{0:T(256)S(1)} %bitcast.590, ...), kind=kLoop, calls=%fused_computation.170 | loop fusion | flops 12975360 | bytes 1349632 | tf_op jit(solution)/shard_map/transpose(jvp(jvp()))/checkpoint/reduce_sum | solution.py:59
  136.4 2.8 %multiply_reduce_fusion.20 = (f32[256]{0:T(256)S(1)}, f32[4,8,8,256]{3,2,1,0:T(8,128)S(1)}, f32[256]{0:T(256)S(1)}, f32[256]{0:T(256)S(1)}, f32[4,8,8,256]{3,2,1,0:T(8,128)S(1)}) fusion(f32[4,8,8,8]{3,2,1,0:T(8,128)S(1)} %get-tuple-element.562, f32[256]{0:T(256)S(1)} %bitcast.586, f32[256]{0:T(256)S(1)} %bitcast.587, ...), kind=kLoop, calls=%fused_computation.164 | loop fusion | flops 12975360 | bytes 1349632 | tf_op jit(solution)/shard_map/transpose(jvp(jvp()))/checkpoint/reduce_sum | solution.py:59
  139.2 2.8 %multiply_reduce_fusion.17 = (f32[256]{0:T(256)S(1)}, f32[4,8,8,256]{3,2,1,0:T(8,128)S(1)}, f32[256]{0:T(256)S(1)}, f32[256]{0:T(256)S(1)}, f32[4,8,8,256]{3,2,1,0:T(8,128)S(1)}) fusion(f32[4,8,8,8]{3,2,1,0:T(8,128)S(1)} %get-tuple-element.564, f32[256]{0:T(256)S(1)} %bitcast.583, f32[256]{0:T(256)S(1)} %bitcast.584, ...), kind=kLoop, calls=%fused_computation.161 | loop fusion | flops 12975360 | bytes 1349632 | tf_op jit(solution)/shard_map/transpose(jvp(jvp()))/checkpoint/reduce_sum | solution.py:59
  142.0 2.8 %multiply_reduce_fusion.14 = (f32[256]{0:T(256)S(1)}, f32[4,8,8,256]{3,2,1,0:T(8,128)S(1)}, f32[256]{0:T(256)S(1)}, f32[256]{0:T(256)S(1)}, f32[4,8,8,256]{3,2,1,0:T(8,128)S(1)}) fusion(f32[4,8,8,8]{3,2,1,0:T(8,128)S(1)} %get-tuple-element.566, f32[256]{0:T(256)S(1)} %bitcast.577, f32[256]{0:T(256)S(1)} %bitcast.578, ...), kind=kLoop, calls=%fused_computation.158 | loop fusion | flops 12975360 | bytes 1349632 | tf_op jit(solution)/shard_map/transpose(jvp(jvp()))/checkpoint/reduce_sum | solution.py:59
  144.8 2.8 %multiply_reduce_fusion.11 = (f32[256]{0:T(256)S(1)}, f32[4,8,8,256]{3,2,1,0:T(8,128)S(1)}, f32[256]{0:T(256)S(1)}, f32[256]{0:T(256)S(1)}, f32[4,8,8,256]{3,2,1,0:T(8,128)S(1)}) fusion(f32[4,8,8,8]{3,2,1,0:T(8,128)S(1)} %get-tuple-element.568, f32[256]{0:T(256)S(1)} %bitcast.574, f32[256]{0:T(256)S(1)} %bitcast.575, ...), kind=kLoop, calls=%fused_computation.155 | loop fusion | flops 12975360 | bytes 1349632 | tf_op jit(solution)/shard_map/transpose(jvp(jvp()))/checkpoint/reduce_sum | solution.py:59
  147.6 2.8 %multiply_reduce_fusion.8 = (f32[256]{0:T(256)S(1)}, f32[4,8,8,256]{3,2,1,0:T(8,128)S(1)}, f32[256]{0:T(256)S(1)}, f32[256]{0:T(256)S(1)}, f32[4,8,8,256]{3,2,1,0:T(8,128)S(1)}) fusion(f32[4,8,8,8]{3,2,1,0:T(8,128)S(1)} %get-tuple-element.570, f32[256]{0:T(256)S(1)} %bitcast.568, f32[256]{0:T(256)S(1)} %bitcast.569, ...), kind=kLoop, calls=%fused_computation.152 | loop fusion | flops 12975360 | bytes 1349632 | tf_op jit(solution)/shard_map/transpose(jvp(jvp()))/checkpoint/reduce_sum | solution.py:59
  150.4 2.8 %multiply_reduce_fusion.5 = (f32[256]{0:T(256)S(1)}, f32[4,8,8,256]{3,2,1,0:T(8,128)S(1)}, f32[256]{0:T(256)S(1)}, f32[256]{0:T(256)S(1)}, f32[4,8,8,256]{3,2,1,0:T(8,128)S(1)}) fusion(f32[4,8,8,8]{3,2,1,0:T(8,128)S(1)} %get-tuple-element.572, f32[256]{0:T(256)S(1)} %bitcast.565, f32[256]{0:T(256)S(1)} %bitcast.566, ...), kind=kLoop, calls=%fused_computation.149 | loop fusion | flops 12975360 | bytes 1349632 | tf_op jit(solution)/shard_map/transpose(jvp(jvp()))/checkpoint/reduce_sum | solution.py:59
  153.2 2.8 %multiply_reduce_fusion.2 = (f32[256]{0:T(256)S(1)}, f32[4,8,8,256]{3,2,1,0:T(8,128)S(1)}, f32[256]{0:T(256)S(1)}, f32[256]{0:T(256)S(1)}, f32[4,8,8,256]{3,2,1,0:T(8,128)S(1)}) fusion(f32[4,8,8,8]{3,2,1,0:T(8,128)S(1)} %get-tuple-element.574, f32[256]{0:T(256)S(1)} %bitcast.559, f32[256]{0:T(256)S(1)} %bitcast.560, ...), kind=kLoop, calls=%fused_computation.146 | loop fusion | flops 12975360 | bytes 1349632 | tf_op jit(solution)/shard_map/transpose(jvp(jvp()))/checkpoint/reduce_sum | solution.py:59
  156.8 1.0 fusion.36
  158.6 2.8 collective-permute-done.21
  161.5 0.9 fusion.41
  162.5 2.1 collective-permute-start.23
  164.6 0.9 collective-permute-done.22
  165.4 2.8 %collective-permute-done.23 = bf16[8,8,256]{2,1,0:T(8,128)(2,1)S(1)} collective-permute-done((bf16[8,8,256]{2,1,0:T(8,128)(2,1)S(1)}, bf16[8,8,256]{2,1,0:T(8,128)(2,1)S(1)}, u32[]{:S(2)}, u32[]{:S(2)}) %collective-permute-start.23) | collective-permute-done | bytes 32800 | tf_op jit(solution)/shard_map/ppermute | solution.py:26
  168.5 0.9 fusion.40
  169.6 31.0 %all-reduce.72 = (f32[3,256]{1,0:T(4,128)}, f32[256]{0:T(256)}) all-reduce(f32[3,256]{1,0:T(4,128)S(1)} %add_add_fusion.4, f32[256]{0:T(256)S(1)} %add.2491), channel_id=1, replica_groups=mesh['groups'=2,'gx'=4,'gy'=4] {'gx','gy'}, use_global_device_ids=true, to_apply=%region_122.123 | all-reduce | flops 1024 | bytes 8192 | tf_op jit(solution)/shard_map/psum | solution.py:224
  201.0 0.9 fusion.46
  201.9 63.2 %all-reduce.76.cloned.1.call-done = (f32[256,256]{1,0:T(8,128)}, f32[256,256]{1,0:T(8,128)}, f32[256,256]{1,0:T(8,128)}, f32[256,256]{1,0:T(8,128)}, f32[256,256]{1,0:T(8,128)}, /*index=5*/f32[256,256]{1,0:T(8,128)}) async-done(((f32[256,256]{1,0:T(8,128)}, f32[256,256]{1,0:T(8,128)}, f32[256,256]{1,0:T(8,128)}, f32[256,256]{1,0:T(8,128)}, f32[256,256]{1,0:T(8,128)}, /*index=5*/f32[256,256]{1,0:T(8,128)}), ...) | async-done | bytes 1572880 | tf_op jit(solution)/shard_map/psum | solution.py:224
  265.1 1.7 copy.93
  266.8 0.7 copy.94
  (217 shorter events, 21.0 us)
Async XLA Ops:
  7.2 43.3 %copy-start = (bf16[256,256]{1,0:T(8,128)(2,1)S(1)}, bf16[256,256]{1,0:T(8,128)(2,1)}, u32[]{:S(2)}) copy-start(bf16[256,256]{1,0:T(8,128)(2,1)} %param.37) | copy-start | bytes 393220
  7.2 11.9 %copy-start.14 = (bf16[4,8,8,2]{2,3,1,0:T(2,128)(2,1)S(1)}, bf16[4,8,8,2]{2,3,1,0:T(2,128)(2,1)}, u32[]{:S(2)}) copy-start(bf16[4,8,8,2]{2,3,1,0:T(2,128)(2,1)} %param.29) | copy-start | bytes 3076
  7.2 11.9 %copy-start.1 = (bf16[4,8,8,256]{3,2,1,0:T(8,128)(2,1)S(1)}, bf16[4,8,8,256]{3,2,1,0:T(8,128)(2,1)}, u32[]{:S(2)}) copy-start(bf16[4,8,8,256]{3,2,1,0:T(8,128)(2,1)} %param.28) | copy-start | bytes 393220
  7.2 11.9 %copy-start.5 = (bf16[256,256]{1,0:T(8,128)(2,1)S(1)}, bf16[256,256]{1,0:T(8,128)(2,1)}, u32[]{:S(2)}) copy-start(bf16[256,256]{1,0:T(8,128)(2,1)} %param.32) | copy-start | bytes 393220
  7.2 257.9 %all-reduce.76.cloned.1.call-start = ((), (), s32[]{:S(2)}) async-start(), calls=%async_computation | async-start | bytes 3145728 | tf_op jit(solution)/shard_map/psum | solution.py:224
  8.1 11.4 %collective-permute-start = (bf16[1,8,8]{2,1,0:T(8,128)(2,1)S(1)}, bf16[1,8,8]{2,1,0:T(8,128)(2,1)S(1)}, u32[]{:S(2)}, u32[]{:S(2)}) collective-permute-start(bf16[1,8,8]{2,1,0:T(8,128)(2,1)S(1)} %get-tuple-element.799), channel_id=1, source_target_pairs={{0,4},{4,8},{8,12},{12,0},{1,5},{5,9},{9,13},{13,1},{2,6},{6,10},{... | collective-permute-start | bytes 392 | tf_op jit(solution)/shard_map/ppermute | solution.py:36
  11.2 8.4 %collective-permute-start.1 = (bf16[1,8,8]{2,1,0:T(8,128)(2,1)S(1)}, bf16[1,8,8]{2,1,0:T(8,128)(2,1)S(1)}, u32[]{:S(2)}, u32[]{:S(2)}) collective-permute-start(bf16[1,8,8]{2,1,0:T(8,128)(2,1)S(1)} %get-tuple-element.800), channel_id=1, source_target_pairs={{4,0},{8,4},{12,8},{0,12},{5,1},{9,5},{13,9},{1,13},{6,2},{10,6},{... | collective-permute-start | bytes 392 | tf_op jit(solution)/shard_map/ppermute | solution.py:38
  13.9 12.5 %collective-permute-start.4 = (bf16[1,8,8,2]{2,3,1,0:T(2,128)(2,1)S(1)}, bf16[1,8,8,2]{2,3,1,0:T(2,128)(2,1)S(1)}, u32[]{:S(2)}, u32[]{:S(2)}) collective-permute-start(bf16[1,8,8,2]{2,3,1,0:T(2,128)(2,1)S(1)} %get-tuple-element.796), channel_id=1, source_target_pairs={{0,4},{4,8},{8,12},{12,0},{1,5},{5,9},{9,13},{13,1},{2,6},{6,10},{... | collective-permute-start | bytes 776 | tf_op jit(solution)/shard_map/ppermute | solution.py:36
  14.0 5.3 %copy-start.8 = (f32[3,256]{1,0:T(4,128)S(1)}, f32[3,256]{1,0:T(4,128)}, u32[]{:S(2)}) copy-start(f32[3,256]{1,0:T(4,128)} %param.38) | copy-start | bytes 9220
  14.0 5.3 %copy-start.6 = (bf16[256,256]{1,0:T(8,128)(2,1)S(1)}, bf16[256,256]{1,0:T(8,128)(2,1)}, u32[]{:S(2)}) copy-start(bf16[256,256]{1,0:T(8,128)(2,1)} %param.35) | copy-start | bytes 393220
  14.0 12.5 %collective-permute-start.5 = (bf16[1,8,8,2]{2,3,1,0:T(2,128)(2,1)S(1)}, bf16[1,8,8,2]{2,3,1,0:T(2,128)(2,1)S(1)}, u32[]{:S(2)}, u32[]{:S(2)}) collective-permute-start(bf16[1,8,8,2]{2,3,1,0:T(2,128)(2,1)S(1)} %get-tuple-element.795), channel_id=1, source_target_pairs={{4,0},{8,4},{12,8},{0,12},{5,1},{9,5},{13,9},{1,13},{6,2},{10,6},{... | collective-permute-start | bytes 776 | tf_op jit(solution)/shard_map/ppermute | solution.py:38
  19.0 11.7 %collective-permute-start.8 = (bf16[1,8,8,256]{3,2,1,0:T(8,128)(2,1)S(1)}, bf16[1,8,8,256]{3,2,1,0:T(8,128)(2,1)S(1)}, u32[]{:S(2)}, u32[]{:S(2)}) collective-permute-start(bf16[1,8,8,256]{3,2,1,0:T(8,128)(2,1)S(1)} %get-tuple-element.555), channel_id=1, source_target_pairs={{0,4},{4,8},{8,12},{12,0},{1,5},{5,9},{9,13},{13,1},{2,6},{6,10},{... | collective-permute-start | bytes 98312 | tf_op jit(solution)/shard_map/ppermute | solution.py:36
  19.6 3.1 %collective-permute-start.2 = (bf16[6,1,8]{2,1,0:T(2,128)(2,1)S(1)}, bf16[6,1,8]{2,1,0:T(2,128)(2,1)S(1)}, u32[]{:S(2)}, u32[]{:S(2)}) collective-permute-start(bf16[6,1,8]{2,1,0:T(2,128)(2,1)S(1)} %get-tuple-element.797), channel_id=1, source_target_pairs={{0,1},{1,2},{2,3},{3,0},{4,5},{5,6},{6,7},{7,4},{8,9},{9,10},{10,1... | collective-permute-start | bytes 296 | tf_op jit(solution)/shard_map/ppermute | solution.py:36
  19.7 6.8 %collective-permute-start.3 = (bf16[6,1,8]{2,1,0:T(2,128)(2,1)S(1)}, bf16[6,1,8]{2,1,0:T(2,128)(2,1)S(1)}, u32[]{:S(2)}, u32[]{:S(2)}) collective-permute-start(bf16[6,1,8]{2,1,0:T(2,128)(2,1)S(1)} %get-tuple-element.798), channel_id=1, source_target_pairs={{1,0},{2,1},{3,2},{0,3},{5,4},{6,5},{7,6},{4,7},{9,8},{10,9},{11,1... | collective-permute-start | bytes 296 | tf_op jit(solution)/shard_map/ppermute | solution.py:38
  22.7 8.0 %collective-permute-start.9 = (bf16[1,8,8,256]{3,2,1,0:T(8,128)(2,1)S(1)}, bf16[1,8,8,256]{3,2,1,0:T(8,128)(2,1)S(1)}, u32[]{:S(2)}, u32[]{:S(2)}) collective-permute-start(bf16[1,8,8,256]{3,2,1,0:T(8,128)(2,1)S(1)} %get-tuple-element.556), channel_id=1, source_target_pairs={{4,0},{8,4},{12,8},{0,12},{5,1},{9,5},{13,9},{1,13},{6,2},{10,6},{... | collective-permute-start | bytes 98312 | tf_op jit(solution)/shard_map/ppermute | solution.py:38
  26.6 3.1 %collective-permute-start.6 = (bf16[6,1,8,2]{2,3,1,0:T(2,128)(2,1)S(1)}, bf16[6,1,8,2]{2,3,1,0:T(2,128)(2,1)S(1)}, u32[]{:S(2)}, u32[]{:S(2)}) collective-permute-start(bf16[6,1,8,2]{2,3,1,0:T(2,128)(2,1)S(1)} %get-tuple-element.787), channel_id=1, source_target_pairs={{0,1},{1,2},{2,3},{3,0},{4,5},{5,6},{6,7},{7,4},{8,9},{9,10},{10,1... | collective-permute-start | bytes 584 | tf_op jit(solution)/shard_map/ppermute | solution.py:36
  26.7 3.1 %collective-permute-start.7 = (bf16[6,1,8,2]{2,3,1,0:T(2,128)(2,1)S(1)}, bf16[6,1,8,2]{2,3,1,0:T(2,128)(2,1)S(1)}, u32[]{:S(2)}, u32[]{:S(2)}) collective-permute-start(bf16[6,1,8,2]{2,3,1,0:T(2,128)(2,1)S(1)} %get-tuple-element.788), channel_id=1, source_target_pairs={{1,0},{2,1},{3,2},{0,3},{5,4},{6,5},{7,6},{4,7},{9,8},{10,9},{11,1... | collective-permute-start | bytes 584 | tf_op jit(solution)/shard_map/ppermute | solution.py:38
  30.7 3.3 %collective-permute-start.10 = (bf16[6,1,8,256]{3,2,1,0:T(8,128)(2,1)S(1)}, bf16[6,1,8,256]{3,2,1,0:T(8,128)(2,1)S(1)}, u32[]{:S(2)}, u32[]{:S(2)}) collective-permute-start(bf16[6,1,8,256]{3,2,1,0:T(8,128)(2,1)S(1)} %get-tuple-element.551), channel_id=1, source_target_pairs={{0,1},{1,2},{2,3},{3,0},{4,5},{5,6},{6,7},{7,4},{8,9},{9,10},{10,1... | collective-permute-start | bytes 73736 | tf_op jit(solution)/shard_map/ppermute | solution.py:36
  32.5 1.6 collective-permute-start.11
  49.2 0.9 copy-start.3
  49.2 1.1 copy-start.4
  50.5 0.7 copy-start.15
  50.8 0.9 copy-start.2
  51.9 5.8 %collective-permute-start.12 = (bf16[1,8,8,256]{3,2,1,0:T(8,128)(2,1)S(1)}, bf16[1,8,8,256]{3,2,1,0:T(8,128)(2,1)S(1)}, u32[]{:S(2)}, u32[]{:S(2)}) collective-permute-start(bf16[1,8,8,256]{3,2,1,0:T(8,128)(2,1)S(1)} %get-tuple-element.553), channel_id=1, source_target_pairs={{0,4},{4,8},{8,12},{12,0},{1,5},{5,9},{9,13},{13,1},{2,6},{6,10},{... | collective-permute-start | bytes 98312 | tf_op jit(solution)/shard_map/ppermute | solution.py:36
  52.0 5.7 %collective-permute-start.13 = (bf16[1,8,8,256]{3,2,1,0:T(8,128)(2,1)S(1)}, bf16[1,8,8,256]{3,2,1,0:T(8,128)(2,1)S(1)}, u32[]{:S(2)}, u32[]{:S(2)}) collective-permute-start(bf16[1,8,8,256]{3,2,1,0:T(8,128)(2,1)S(1)} %get-tuple-element.554), channel_id=1, source_target_pairs={{4,0},{8,4},{12,8},{0,12},{5,1},{9,5},{13,9},{1,13},{6,2},{10,6},{... | collective-permute-start | bytes 98312 | tf_op jit(solution)/shard_map/ppermute | solution.py:38
  57.7 3.3 %collective-permute-start.14 = (bf16[6,1,8,256]{3,2,1,0:T(8,128)(2,1)S(1)}, bf16[6,1,8,256]{3,2,1,0:T(8,128)(2,1)S(1)}, u32[]{:S(2)}, u32[]{:S(2)}) collective-permute-start(bf16[6,1,8,256]{3,2,1,0:T(8,128)(2,1)S(1)} %get-tuple-element.549), channel_id=1, source_target_pairs={{0,1},{1,2},{2,3},{3,0},{4,5},{5,6},{6,7},{7,4},{8,9},{9,10},{10,1... | collective-permute-start | bytes 73736 | tf_op jit(solution)/shard_map/ppermute | solution.py:36
  58.4 2.7 collective-permute-start.15
  76.9 0.9 copy-start.7
  107.7 3.3 %collective-permute-start.16 = (bf16[6,8,256]{2,1,0:T(8,128)(2,1)S(1)}, bf16[6,8,256]{2,1,0:T(8,128)(2,1)S(1)}, u32[]{:S(2)}, u32[]{:S(2)}) collective-permute-start(bf16[6,8,256]{2,1,0:T(8,128)(2,1)S(1)} %get-tuple-element.544), channel_id=1, source_target_pairs={{1,0},{2,1},{3,2},{0,3},{5,4},{6,5},{7,6},{4,7},{9,8},{10,9},{11,1... | collective-permute-start | bytes 73736 | tf_op jit(solution)/shard_map/ppermute | solution.py:26
  109.5 3.3 %collective-permute-start.17 = (bf16[6,8,256]{2,1,0:T(8,128)(2,1)S(1)}, bf16[6,8,256]{2,1,0:T(8,128)(2,1)S(1)}, u32[]{:S(2)}, u32[]{:S(2)}) collective-permute-start(bf16[6,8,256]{2,1,0:T(8,128)(2,1)S(1)} %get-tuple-element.543), channel_id=1, source_target_pairs={{3,0},{0,1},{1,2},{2,3},{7,4},{4,5},{5,6},{6,7},{11,8},{8,9},{9,10... | collective-permute-start | bytes 73736 | tf_op jit(solution)/shard_map/ppermute | solution.py:26
  112.8 5.5 %collective-permute-start.18 = (bf16[8,8,256]{2,1,0:T(8,128)(2,1)S(1)}, bf16[8,8,256]{2,1,0:T(8,128)(2,1)S(1)}, u32[]{:S(2)}, u32[]{:S(2)}) collective-permute-start(bf16[8,8,256]{2,1,0:T(8,128)(2,1)S(1)} %get-tuple-element.548), channel_id=1, source_target_pairs={{4,0},{8,4},{12,8},{0,12},{5,1},{9,5},{13,9},{1,13},{6,2},{10,6},{... | collective-permute-start | bytes 98312 | tf_op jit(solution)/shard_map/ppermute | solution.py:26
  117.0 5.8 %collective-permute-start.19 = (bf16[8,8,256]{2,1,0:T(8,128)(2,1)S(1)}, bf16[8,8,256]{2,1,0:T(8,128)(2,1)S(1)}, u32[]{:S(2)}, u32[]{:S(2)}) collective-permute-start(bf16[8,8,256]{2,1,0:T(8,128)(2,1)S(1)} %get-tuple-element.547), channel_id=1, source_target_pairs={{12,0},{0,4},{4,8},{8,12},{13,1},{1,5},{5,9},{9,13},{14,2},{2,6},{... | collective-permute-start | bytes 98312 | tf_op jit(solution)/shard_map/ppermute | solution.py:26
  156.2 2.4 collective-permute-start.20
  158.1 3.3 %collective-permute-start.21 = (bf16[6,8,256]{2,1,0:T(8,128)(2,1)S(1)}, bf16[6,8,256]{2,1,0:T(8,128)(2,1)S(1)}, u32[]{:S(2)}, u32[]{:S(2)}) collective-permute-start(bf16[6,8,256]{2,1,0:T(8,128)(2,1)S(1)} %get-tuple-element.541), channel_id=1, source_target_pairs={{3,0},{0,1},{1,2},{2,3},{7,4},{4,5},{5,6},{6,7},{11,8},{8,9},{9,10... | collective-permute-start | bytes 73736 | tf_op jit(solution)/shard_map/ppermute | solution.py:26
  161.5 4.0 %collective-permute-start.22 = (bf16[8,8,256]{2,1,0:T(8,128)(2,1)S(1)}, bf16[8,8,256]{2,1,0:T(8,128)(2,1)S(1)}, u32[]{:S(2)}, u32[]{:S(2)}) collective-permute-start(bf16[8,8,256]{2,1,0:T(8,128)(2,1)S(1)} %get-tuple-element.546), channel_id=1, source_target_pairs={{4,0},{8,4},{12,8},{0,12},{5,1},{9,5},{13,9},{1,13},{6,2},{10,6},{... | collective-permute-start | bytes 98312 | tf_op jit(solution)/shard_map/ppermute | solution.py:26
  162.5 5.8 %collective-permute-start.23 = (bf16[8,8,256]{2,1,0:T(8,128)(2,1)S(1)}, bf16[8,8,256]{2,1,0:T(8,128)(2,1)S(1)}, u32[]{:S(2)}, u32[]{:S(2)}) collective-permute-start(bf16[8,8,256]{2,1,0:T(8,128)(2,1)S(1)} %get-tuple-element.545), channel_id=1, source_target_pairs={{12,0},{0,4},{4,8},{8,12},{13,1},{1,5},{5,9},{9,13},{14,2},{2,6},{... | collective-permute-start | bytes 98312 | tf_op jit(solution)/shard_map/ppermute | solution.py:26
  265.1 1.7 copy-start.13
  265.1 2.4 copy-start.12
  266.8 1.4 copy-start.11
  267.6 1.4 copy-start.10
  268.3 1.4 copy-start.9
Sparse Core Ops, SparseCore 0:
  169.6 95.4 all-reduce.75
where the time goes:
time: 278 us; the launch traced here: 277 us
  other arithmetic  89.2 us (32%)
  waiting for transfers between devices  84.9 us (31%)
  starting transfers between devices  32.7 us (12%)
  blocking collectives  31 us (11%)
  between operations  15.6 us (6%)
  matrix products  14.8 us (5%)
  local copies, waits for them, and re-layouts  9.06 us (3%)
    psum x1, waiting for transfers between devices, per_device(): totals = lax.psum(totals, ('gx', 'gy'))  63.2 us
    reduce_sum x18, other arithmetic, pair_row(): dist_sq[..., None] * geometry[2]  50.6 us
    psum x1, blocking collectives, per_device(): totals = lax.psum(totals, ('gx', 'gy'))  31 us
    reduce_sum x6, other arithmetic, pair_row(): return jnp.sum(pair_weight[..., None] * jax.nn.silu(preact), axis=-2)  29.9 us
    ppermute x8, starting transfers between devices, extended(): lax.ppermute(head, axis, [((i + 1) % count, i) for i in range(count)])  18.1 us
    ppermute x8, waiting for transfers between devices, passed_along(): return lax.ppermute(block, axis, route)  14.6 us
    ppermute x8, starting transfers between devices, passed_along(): return lax.ppermute(block, axis, route)  8.78 us
    dot_general x12, matrix products, outer_sum(): lax.dot_general(inputs16.reshape(-1, inputs16.shape[-1]).astype(jnp.float...  7.89 us
  transfers between devices with their start and end apart: 25, of which 13 were waited for; matrix products, arithmetic and copies ran while one was open for 3% of the time, Pallas kernels for 0%

commit v1 on v0

v1 whole, which is shorter than its diff:
```python
from functools import partial

import jax
import jax.numpy as jnp
from jax import lax
from jax.experimental import pallas as pl
from jax.experimental.pallas import tpu as pltpu
from jax.sharding import PartitionSpec as P

STEPS = 2
EPSILON = 1e-05
OFFSETS = ((-1, -1), (-1, 0), (-1, 1), (0, -1), (0, 0), (0, 1), (1, -1), (1, 0), (1, 1))
SIDES = ((1, 0), (-1, 0), (0, 1), (0, -1), (1, 1), (1, -1), (-1, 1), (-1, -1))
MESH = pl.DeviceIdType.MESH
F32 = jnp.float32
BF16 = jnp.bfloat16
SEND_AT = 16
GEO_AT = 88
DEPTH = 128


def round16(rows):
    return -(-rows // 16) * 16


def mm(a, b):
    return jnp.dot(a.astype(BF16), b.astype(BF16), preferred_element_type=F32)


def mm_t(a, b):
    return lax.dot_general(
        a.astype(BF16), b.astype(BF16), (((1,), (1,)), ((), ())), preferred_element_type=F32
    )


def outer(a, b):
    return lax.dot_general(
        a.astype(BF16), b.astype(BF16), (((0,), (0,)), ((), ())), preferred_element_type=F32
    )


def rounded(value):
    return value.astype(BF16).astype(F32)


def segments(cx, cy, slots):
    found, at = [], 0
    for dx, dy in SIDES:
        rows = round16((cx if dx == 0 else 1) * (cy if dy == 0 else 1) * slots)
        found.append((at, rows))
        at += rows
    return found, at


def span(step, size, low, high):
    if step == 0:
        return range(1, size + 1)
    return [high] if step == 1 else [low]


def kernel(
    ngx,
    ngy,
    cells_x,
    cells_y,
    h_ref,
    cell_ref,
    cot_ref,
    w_recv,
    w_send,
    w_msg,
    w_nh,
    w_nm,
    w_out,
    geom_ref,
    gain_ref,
    latent_out,
    grad_latent,
    out_a,
    out_b,
    ext,
    gext,
    recv,
    agg,
    g_agg,
    g_recv,
    hs,
    agg16,
    msg16,
    act16,
    hidden,
    xhat,
    rstd,
    acc,
    acc_small,
    acc_geo,
    pos_send,
    pos_recv,
    pos_ext,
    feat,
    geo,
    mat,
    mat_t,
    weight,
    geo_b,
    halo_send,
    halo_recv,
    part_a,
    part_b,
    got_a,
    got_b,
    pos_sems,
    halo_sems,
    red_sems,
):
    slots = 8
    cells = cells_x * cells_y
    pairs = 9 * slots * slots
    wide = geo.shape[-1]
    n = ngx * ngy
    gx, gy = lax.axis_index("gx"), lax.axis_index("gy")
    me = gx * ngy + gy
    width = h_ref.shape[1]
    segs, _ = segments(cells_x, cells_y, slots)

    def place(dx, dy):
        return {"gx": lax.rem(gx + dx + ngx, ngx), "gy": lax.rem(gy + dy + ngy, ngy)}

    def peer(k):
        other = lax.rem(me + k, n)
        return other, {"gx": lax.div(other, ngy), "gy": lax.rem(other, ngy)}

    barrier = pltpu.get_barrier_semaphore()

    def greet(k, carry):
        _, device = peer(k)
        pl.semaphore_signal(barrier, inc=1, device_id=device, device_id_type=MESH)
        return carry

    lax.fori_loop(1, n, greet, 0)

    def wait_all(ref, sem):
        pltpu.make_async_copy(ref, ref, sem).wait()

    by_cell = cell_ref[...]
    for d, (dx, dy) in enumerate(SIDES):
        xs = [x - 1 for x in span(dx, cells_x, 1, cells_x)]
        if dx != 0 and dy == 0:
            pos_send[d] = by_cell[xs[0]]
        else:
            y = 0 if dy == -1 else cells_y - 1
            rows = [by_cell[x, y : y + 1] for x in xs]
            rows += [rows[-1]] * (cells_y - len(rows))
            pos_send[d] = jnp.concatenate(rows, axis=0)

    h0 = h_ref[...]
    pl.semaphore_wait(barrier, n - 1)
    for d, (dx, dy) in enumerate(SIDES):
        pltpu.make_async_remote_copy(
            pos_send.at[d], pos_recv.at[d], pos_sems.at[0], pos_sems.at[1],
            device_id=place(dx, dy), device_id_type=MESH,
        ).start()

    def start_halo(phase, taken):
        for d, (dx, dy) in enumerate(SIDES):
            at, rows = segs[d]
            tiles = taken(dx, dy)
            tiles = tiles + [tiles[-1]] * (rows // slots - len(tiles))
            halo_send[phase, pl.ds(at, rows)] = jnp.concatenate(tiles, axis=0).astype(BF16)
            pltpu.make_async_remote_copy(
                halo_send.at[phase, pl.ds(at, rows)],
                halo_recv.at[phase, pl.ds(at, rows)],
                halo_sems.at[0, phase],
                halo_sems.at[1, phase],
                device_id=place(dx, dy),
                device_id_type=MESH,
            ).start()

    def end_halo(phase):
        wait_all(halo_recv.at[phase], halo_sems.at[1, phase])
        wait_all(halo_send.at[phase], halo_sems.at[0, phase])

    def project(step, h):
        hs[step] = h
        recv[step] = mm(h, w_recv[...]).reshape(cells, slots, width)
        half = (rounded(mm(h, w_send[...])) * 0.5).reshape(cells_x, cells_y, slots, width)

        def taken(dx, dy):
            return [
                half[x - 1, y - 1]
                for x in span(dx, cells_x, 1, cells_x)
                for y in span(dy, cells_y, 1, cells_y)
            ]

        start_halo(step, taken)
        for x in range(cells_x):
            ext[step, x + 1, pl.ds(1, cells_y)] = half[x]

    def arrive(step):
        end_halo(step)
        for d, (dx, dy) in enumerate(SIDES):
            at, rows = segs[d]
            block = halo_recv[step, pl.ds(at, rows)].astype(F32)
            where = [
                (x, y)
                for x in span(dx, cells_x, cells_x + 1, 0)
                for y in span(dy, cells_y, cells_y + 1, 0)
            ]
            for t, (x, y) in enumerate(where):
                ext[step, x, y] = block[t * slots : (t + 1) * slots]

    project(0, h0)

    g = geom_ref[...] * 0.5
    g_hi = rounded(g)
    g_lo = g - g_hi
    rows = []
    for f in range(3):
        rows += [g_hi[f : f + 1], g_hi[f : f + 1], g_lo[f : f + 1]]
    rows.append(jnp.zeros((DEPTH - GEO_AT - 9, width), F32))
    geo_b[...] = jnp.concatenate(rows, axis=0)

    k_at = lax.broadcasted_iota(jnp.int32, (DEPTH, wide), 0)
    r_at = lax.broadcasted_iota(jnp.int32, (DEPTH, wide), 1)
    takes_recv = (k_at < SEND_AT) & ((r_at & 7) == (k_at & 7))
    takes_send = (k_at >= SEND_AT) & (k_at < GEO_AT) & ((r_at >> 3) == k_at - SEND_AT)
    one_hot = jnp.where((r_at < pairs) & (takes_recv | takes_send), 1.0, 0.0).astype(F32)
    lane = lax.broadcasted_iota(jnp.int32, (1, wide), 1)
    cell_o = lane >> 6
    third = (cell_o >= 3).astype(jnp.int32) + (cell_o >= 6).astype(jnp.int32)
    off_x = (third - 1).astype(F32)
    off_y = (cell_o - third * 3 - 1).astype(F32)
    same = (cell_o == 4) & (((lane >> 3) & 7) == (lane & 7))

    wait_all(pos_recv, pos_sems.at[1])
    wait_all(pos_send, pos_sems.at[0])
    for x in range(cells_x):
        pos_ext[x + 1, pl.ds(1, cells_y)] = by_cell[x]
    for d, (dx, dy) in enumerate(SIDES):
        tile = pos_recv[d]
        xs = list(span(dx, cells_x, cells_x + 1, 0))
        if dx != 0 and dy == 0:
            pos_ext[xs[0], pl.ds(1, cells_y)] = tile
        else:
            y = 0 if dy == 1 else cells_y + 1
            for t, x in enumerate(xs):
                pos_ext[x, pl.ds(y, 1)] = tile[t : t + 1]
    feat[...] = jnp.zeros(feat.shape, F32)
    for x in range(cells_x):
        rows_x = pl.ds(x * cells_y, cells_y)
        for f in range(3):
            own = by_cell[x][:, f * slots : (f + 1) * slots]
            feat[f, rows_x, 0:slots] = own if f == 2 else -own
        for o, (ox, oy) in enumerate(OFFSETS):
            near = pos_ext[x + 1 + ox, pl.ds(1 + oy, cells_y)]
            at = SEND_AT + o * slots
            for f in range(3):
                feat[f, rows_x, at : at + slots] = near[:, f * slots : (f + 1) * slots]
    disp_x = mm(feat[0], one_hot) + off_x
    disp_y = mm(feat[1], one_hot) + off_y
    both = mm(feat[2], one_hot)
    dist = disp_x * disp_x + disp_y * disp_y
    wgt = jnp.where((both > 1.5) & jnp.logical_not(same), 1.0 / (1.0 + dist), 0.0)
    for f, value in enumerate((disp_x, disp_y, dist, wgt)):
        geo[f] = value
    spread_row = lax.broadcasted_iota(jnp.int32, (DEPTH, 128), 0)
    spreads = ((spread_row == GEO_AT + 9) | (spread_row == GEO_AT + 10)).astype(F32).astype(BF16)
    row16 = lax.broadcasted_iota(jnp.int32, (16, wide), 0)

    def prepare(c, carry):
        tile = jnp.zeros((16, wide), F32)
        for f in range(4):
            value = geo[f, pl.ds(c, 1)]
            hi = rounded(value)
            lo = value - hi
            at = 3 * f
            if f < 3:
                tile = jnp.where((row16 == at) | (row16 == at + 2), hi, tile)
            else:
                tile = jnp.where(row16 == at, hi, tile)
            tile = jnp.where(row16 == at + 1, lo, tile)
        full = jnp.concatenate(
            [one_hot[:GEO_AT], tile, jnp.zeros((DEPTH - GEO_AT - 16, wide), F32)], axis=0
        )
        mat_t[c] = full[:, :pairs].astype(BF16)
        turned = full.T[:pairs].astype(BF16)
        mat[c] = turned
        weight[c] = jnp.dot(turned, spreads, preferred_element_type=F32)
        return carry

    lax.fori_loop(0, cells, prepare, 0)

    def half_preact(step, c):
        x, y = lax.div(c, cells_y), lax.rem(c, cells_y)
        r = recv[step, c] * 0.5
        hi = rounded(r)
        tiles = [hi, r - hi]
        tiles += [ext[step, x + 1 + ox, y + 1 + oy] for ox, oy in OFFSETS]
        b = jnp.concatenate(tiles + [geo_b[...]], axis=0).astype(BF16)
        return jnp.dot(mat[c], b, preferred_element_type=F32)

    block = slots * slots

    def weights_of(c, o):
        w = weight[c, o * block : (o + 1) * block]
        return jnp.concatenate([w] * (width // 128), axis=1).reshape(slots, slots, width)

    def forward_pairs(step):
        def body(c, carry):
            q = half_preact(step, c)
            total = jnp.zeros((slots, width), F32)
            for o in range(9):
                part = q[o * block : (o + 1) * block].reshape(slots, slots, width)
                total = total + jnp.sum(weights_of(c, o) * (part + part * jnp.tanh(part)), axis=0)
            agg[c] = total
            return carry

        lax.fori_loop(0, cells, body, 0)

    def backward_pairs(step):
        gext[...] = jnp.zeros(gext.shape, F32)

        def body(c, carry):
            x, y = lax.div(c, cells_y), lax.rem(c, cells_y)
            q = half_preact(step, c)
            up = (g_agg[c] * 0.5)[None]
            parts = []
            for o in range(9):
                part = q[o * block : (o + 1) * block].reshape(slots, slots, width)
                t = jnp.tanh(part)
                d = (weights_of(c, o) * up) * ((1.0 + t) * (1.0 + (part - part * t)))
                parts.append(d.reshape(block, width).astype(BF16))
            back = jnp.dot(mat_t[c], jnp.concatenate(parts, axis=0), preferred_element_type=F32)
            g_recv[c] = back[:slots]
            for o, (ox, oy) in enumerate(OFFSETS):
                at = SEND_AT + o * slots
                gext[x + 1 + ox, y + 1 + oy] += back[at : at + slots]
            acc_geo[...] += back[GEO_AT : GEO_AT + 16]
            return carry

        lax.fori_loop(0, cells, body, 0)

    gain = gain_ref[...]

    def node_forward(step):
        a16 = agg[...].reshape(cells * slots, width).astype(BF16)
        agg16[step] = a16
        m16 = mm(a16, w_msg[...]).astype(BF16)
        msg16[step] = m16
        hid = mm(hs[step], w_nh[...]) + mm(m16, w_nm[...])
        hidden[step] = hid
        half = hid * 0.5
        a = (half + half * jnp.tanh(half)).astype(BF16)
        act16[step] = a
        out = mm(a, w_out[...])
        center = out - jnp.mean(out, axis=-1, keepdims=True)
        scale = lax.rsqrt(jnp.mean(center * center, axis=-1, keepdims=True) + EPSILON)
        normed = center * scale
        xhat[step] = normed
        rstd[step] = jnp.broadcast_to(scale, rstd.shape[1:])
        return (hs[step].astype(F32) + normed * gain).astype(BF16)

    arrive(0)
    forward_pairs(0)
    project(1, node_forward(0))
    arrive(1)
    forward_pairs(1)
    latent_out[...] = node_forward(1)

    def spread_out(part, got, share, sem):
        def one(k, carry):
            other, device = peer(k)
            pltpu.make_async_remote_copy(
                part.at[pl.ds(pl.multiple_of(other * share, 16), share)],
                got.at[k - 1],
                red_sems.at[0, sem],
                red_sems.at[1, sem],
                device_id=device,
                device_id_type=MESH,
            ).start()
            return carry

        lax.fori_loop(1, n, one, 0)

    def gather_in(part, got, share, result, sem):
        wait_all(got, red_sems.at[1, sem])
        wait_all(got, red_sems.at[0, sem])
        mine = pl.ds(pl.multiple_of(me * share, 16), share)
        total = lax.fori_loop(
            0, n - 1, lambda k, t: t + got[k].astype(F32), part[mine].astype(F32)
        )
        result[mine] = total.astype(BF16)

        def one(k, carry):
            _, device = peer(k)
            pltpu.make_async_remote_copy(
                result.at[mine], result.at[mine], red_sems.at[0, sem + 1],
                red_sems.at[1, sem + 1], device_id=device, device_id_type=MESH,
            ).start()
            return carry

        lax.fori_loop(1, n, one, 0)

    def gathered(share, result, sem):
        size = result.at[pl.ds(0, (n - 1) * share)]
        wait_all(size, red_sems.at[1, sem + 1])
        wait_all(size, red_sems.at[0, sem + 1])

    share_a = got_a.shape[1]
    share_b = got_b.shape[1]

    flow = cot_ref[...]
    acc_geo[...] = jnp.zeros(acc_geo.shape, F32)
    for step in (1, 0):
        last = step == 0

        def put(index, term):
            if not last:
                acc[index] = term
                return
            term = (acc[index] + term).astype(BF16)
            if index < 4:
                part_a[pl.ds(index * width, width)] = term
            else:
                part_b[pl.ds((index - 4) * width, width)] = term

        flow32 = flow.astype(F32)
        normed = xhat[step]
        g_gain = jnp.sum(flow32 * normed, axis=0, keepdims=True)
        if last:
            g_gain = g_gain + acc_small[0:1]
        acc_small[...] = jnp.broadcast_to(g_gain, acc_small.shape)
        scaled = flow32 * gain
        d_out = rstd[step][:, :1] * (
            scaled
            - jnp.mean(scaled, axis=-1, keepdims=True)
            - normed * jnp.mean(scaled * normed, axis=-1, keepdims=True)
        )
        put(3, outer(act16[step], d_out))
        d_act = rounded(mm_t(d_out, w_out[...]))
        half = hidden[step] * 0.5
        t = jnp.tanh(half)
        d_hid = (d_act * 0.5) * ((1.0 + t) * (1.0 + (half - half * t)))
        put(1, outer(hs[step], d_hid))
        put(2, outer(msg16[step], d_hid))
        d_msg = mm_t(d_hid, w_nm[...]).astype(BF16)
        put(0, outer(agg16[step], d_msg))
        if last:
            if part_a.shape[0] > 4 * width:
                part_a[pl.ds(4 * width, part_a.shape[0] - 4 * width)] = jnp.zeros(
                    (part_a.shape[0] - 4 * width, width), BF16
                )
            spread_out(part_a, got_a, share_a, 0)
        g_agg[...] = rounded(mm_t(d_msg, w_msg[...])).reshape(cells, slots, width)
        backward_pairs(step)

        def taken(dx, dy):
            return [
                gext[x, y]
                for x in span(dx, cells_x, 0, cells_x + 1)
                for y in span(dy, cells_y, 0, cells_y + 1)
            ]

        start_halo(STEPS + step, taken)
        d_recv = g_recv[...].reshape(cells * slots, width)
        put(4, outer(hs[step], d_recv))
        d_h = flow32 + rounded(mm_t(d_hid, w_nh[...])) + rounded(mm_t(d_recv, w_recv[...]))
        if last:
            gather_in(part_a, got_a, share_a, out_a, 0)
        end_halo(STEPS + step)
        for d, (dx, dy) in enumerate(SIDES):
            at, rows_d = segs[d]
            arrived = halo_recv[STEPS + step, pl.ds(at, rows_d)].astype(F32)
            where = [
                (x, y)
                for x in span(dx, cells_x, cells_x, 1)
                for y in span(dy, cells_y, cells_y, 1)
            ]
            for i, (x, y) in enumerate(where):
                gext[x, y] += arrived[i * slots : (i + 1) * slots]
        d_send = jnp.concatenate(
            [
                gext[x + 1, pl.ds(1, cells_y)].reshape(cells_y * slots, width)
                for x in range(cells_x)
            ],
            axis=0,
        ).astype(BF16)
        put(5, outer(hs[step], d_send))
        if last:
            sums = acc_geo[...]
            tail = [sums[3 * f : 3 * f + 1] + sums[3 * f + 1 : 3 * f + 2] for f in range(3)]
            tail.append(acc_small[0:1])
            rest = part_b.shape[0] - 2 * width
            tail.append(jnp.zeros((rest - 4, width), F32))
            part_b[pl.ds(2 * width, rest)] = jnp.concatenate(tail, axis=0).astype(BF16)
            spread_out(part_b, got_b, share_b, 2)
        flow = (d_h + rounded(mm_t(d_send, w_send[...]))).astype(BF16)
    grad_latent[...] = flow
    gather_in(part_b, got_b, share_b, out_b, 2)
    gathered(share_a, out_a, 0)
    gathered(share_b, out_b, 2)


def per_device(
    ngx,
    ngy,
    latent,
    positions,
    counts,
    cotangent,
    w_recv,
    w_send,
    w_msg,
    w_node_h,
    w_node_m,
    w_out,
    geometry,
    gain,
):
    cells_x, cells_y, slots, width = latent.shape
    cells = cells_x * cells_y
    rows = cells * slots
    n = ngx * ngy
    slot_index = lax.broadcasted_iota(jnp.int32, (cells_x, cells_y, slots), 2)
    validity = (slot_index < counts[:, :, None]).astype(F32)
    by_cell = jnp.concatenate(
        [
            positions[..., 0].astype(F32),
            positions[..., 1].astype(F32),
            validity,
            jnp.zeros((cells_x, cells_y, 128 - 3 * slots), F32),
        ],
        axis=-1,
    )
    pairs = 9 * slots * slots
    wide = -(-pairs // 128) * 128
    _, halo_rows = segments(cells_x, cells_y, slots)
    share_a = round16(-(-4 * width // n))
    share_b = round16(-(-(2 * width + 16) // n))
    vmem = pltpu.VMEM
    scratch = [
        vmem((STEPS, cells_x + 2, cells_y + 2, slots, width), F32),
        vmem((cells_x + 2, cells_y + 2, slots, width), F32),
        vmem((STEPS, cells, slots, width), F32),
        vmem((cells, slots, width), F32),
        vmem((cells, slots, width), F32),
        vmem((cells, slots, width), F32),
        vmem((STEPS, rows, width), BF16),
        vmem((STEPS, rows, width), BF16),
        vmem((STEPS, rows, width), BF16),
        vmem((STEPS, rows, width), BF16),
        vmem((STEPS, rows, width), F32),
        vmem((STEPS, rows, width), F32),
        vmem((STEPS, rows, 128), F32),
        vmem((6, width, width), F32),
        vmem((8, width), F32),
        vmem((16, width), F32),
        vmem((8, cells_y, 128), F32),
        vmem((8, cells_y, 128), F32),
        vmem((cells_x + 2, -(-(cells_y + 2) // 8) * 8, 128), F32),
        vmem((3, cells, 128), F32),
        vmem((4, cells, wide), F32),
        vmem((cells, pairs, DEPTH), BF16),
        vmem((cells, DEPTH, pairs), BF16),
        vmem((cells, pairs, 128), F32),
        vmem((DEPTH - GEO_AT, width), F32),
        vmem((2 * STEPS, halo_rows, width), BF16),
        vmem((2 * STEPS, halo_rows, width), BF16),
        vmem((n * share_a, width), BF16),
        vmem((n * share_b, width), BF16),
        vmem((n - 1, share_a, width), BF16),
        vmem((n - 1, share_b, width), BF16),
        pltpu.SemaphoreType.DMA((2,)),
        pltpu.SemaphoreType.DMA((2, 2 * STEPS)),
        pltpu.SemaphoreType.DMA((2, 4)),
    ]
    spec = pl.BlockSpec(memory_space=pltpu.VMEM)
    new, flow, sums_a, sums_b = pl.pallas_call(
        partial(kernel, ngx, ngy, cells_x, cells_y),
        out_shape=[
            jax.ShapeDtypeStruct((rows, width), BF16),
            jax.ShapeDtypeStruct((rows, width), BF16),
            jax.ShapeDtypeStruct((n * share_a, width), BF16),
            jax.ShapeDtypeStruct((n * share_b, width), BF16),
        ],
        in_specs=[spec] * 11,
        out_specs=[spec] * 4,
        scratch_shapes=scratch,
        compiler_params=pltpu.CompilerParams(
            collective_id=0, has_side_effects=True, vmem_limit_bytes=56 * 2**20
        ),
        name="evolver",
    )(
        latent.reshape(rows, width),
        by_cell,
        cotangent.reshape(rows, width),
        w_recv,
        w_send,
        w_msg,
        w_node_h,
        w_node_m,
        w_out,
        geometry,
        gain.reshape(1, width),
    )

    def piece(sums, at, size):
        return sums[at : at + size].astype(F32)

    return (
        new.reshape(latent.shape),
        flow.reshape(latent.shape),
        piece(sums_b, 0, width),
        piece(sums_b, width, width),
        piece(sums_a, 0, width),
        piece(sums_a, width, width),
        piece(sums_a, 2 * width, width),
        piece(sums_a, 3 * width, width),
        piece(sums_b, 2 * width, 3),
        piece(sums_b, 2 * width + 3, 1).reshape(width),
    )


def solution(mesh):
    cell_spec = P(("groups", "gx"), "gy", None, None)
    placed = (cell_spec, cell_spec, P(("groups", "gx"), "gy"), cell_spec) + (P(),) * 8
    return jax.shard_map(
        partial(per_device, mesh.shape["gx"], mesh.shape["gy"]),
        mesh=mesh,
        in_specs=placed,
        out_specs=(cell_spec, cell_spec) + (P("groups", None),) * 7 + (P("groups"),),
        check_vma=False,
    )
```

time: 278 us -> 124 us (0.45)
  Pallas kernels: 0 us -> 113 us
  waiting for transfers between devices: 84.9 us -> 0 us
  other arithmetic: 89.2 us -> 4.87 us
  starting transfers between devices: 32.7 us -> 0 us
  blocking collectives: 31 us -> 0 us
  between operations: 15.6 us -> 0.68 us
  matrix products: 14.8 us -> 0 us
  local copies, waits for them, and re-layouts: 9.06 us -> 3.19 us
    pallas_call x0 -> x1, Pallas kernels: none -> 113 us  [per_device(): pl.pallas_call(partial(kernel, ngx, ngy, cells_x, cells_y), out_shape=[ja...]
    reduce_sum x28 -> x0, other arithmetic: 82.1 us -> none  [the longest x18 50.6 us: pair_row(): dist_sq[..., None] * geometry[2]]
    psum x1 -> x0, waiting for transfers between devices: 63.2 us -> none  [per_device(): totals = lax.psum(totals, ('gx', 'gy'))]
    ppermute x24 -> x0, starting transfers between devices: 32.7 us -> none  [the longest x8 18.1 us: extended(): lax.ppermute(head, axis, [((i + 1) % count, i) for i in range(count)])]
    psum x1 -> x0, blocking collectives: 31 us -> none  [per_device(): totals = lax.psum(totals, ('gx', 'gy'))]
    ppermute x24 -> x0, waiting for transfers between devices: 21.7 us -> none  [the longest x8 14.6 us: passed_along(): return lax.ppermute(block, axis, route)]
    dot_general x36 -> x0, matrix products: 14.8 us -> none  [the longest x12 7.89 us: outer_sum(): lax.dot_general(inputs16.reshape(-1, inputs16.shape[-1]).astype(jnp.float...]
    unnamed x43 -> x10, local copies, waits for them, and re-layouts: 7.25 us -> 2.29 us
  transfers between devices with their start and end apart: 25 -> 0, of which waited for: 13 -> 0; matrix products, arithmetic and copies ran while one was open for 3% -> 0% of each run, Pallas kernels for 0% -> 0%
where the time goes in v1:
time: 124 us; the launch traced here: 121 us
  Pallas kernels  113 us (91%)
  other arithmetic  4.87 us (4%)
  local copies, waits for them, and re-layouts  3.19 us (3%)
    pallas_call x1, Pallas kernels, per_device(): pl.pallas_call(partial(kernel, ngx, ngy, cells_x, cells_y), out_shape=[ja...  113 us
    convert_element_type x3, other arithmetic, piece(): return sums[at:at + size].astype(F32)  3.54 us

profile of v1, /device:TPU:0, one launch (start us, length us, event | category | flops | bytes accessed | tf_op | source)
XLA Modules:
  0.0 121.3 jit_solution(18303074385636151147)
XLA Ops:
  0.6 0.8 fusion.3
  1.5 0.0 copy-start.3
  1.5 0.7 copy-done.3
  2.2 0.1 fusion
  2.2 0.1 pad.3.clone
  2.3 0.7 maximum_maximum_fusion.cell_ref
  3.0 112.6 %evolver.1 = (bf16[256,256]{1,0:T(8,128)(2,1)}, bf16[256,256]{1,0:T(8,128)(2,1)}, bf16[1024,256]{1,0:T(8,128)(2,1)}, bf16[768,256]{1,0:T(8,128)(2,1)}) custom-call(bf16[256,256]{1,0:T(8,128)(2,1)} %bitcast.16, f32[4,8,128]{2,1,0:T(8,128)} %maximum_maximum_fusion.cell_ref, bf16[256,256]{1,0:T(8,128)(2,1)} %bitcast.17, bf16[256,256]{1,0:T(8,128)(2,1)} %w_recv.1, ...), custom_call_target="tpu_custom_call" | custom-call | tf_op jit(solution)/shard_map/evolver/pallas_call | solution.py:578
  115.6 0.0 copy-start
  115.6 2.1 %slice_convert_fusion = (f32[256,256]{1,0:T(8,128)}, f32[256,256]{1,0:T(8,128)}, f32[256,256]{1,0:T(8,128)}, f32[256,256]{1,0:T(8,128)}) fusion(bf16[1024,256]{1,0:T(8,128)(2,1)} %get-tuple-element.17), kind=kLoop, calls=%fused_computation | loop fusion | flops 262144 | bytes 1572864 | tf_op jit(solution)/shard_map/convert_element_type | solution.py:608
  117.7 0.0 copy-done
  117.7 0.0 copy-start.2
  117.7 0.8 slice_convert_fusion.4
  118.6 0.6 slice_convert_fusion.6
  119.2 0.6 slice_convert_fusion.7
  119.7 0.0 copy-done.2
  119.7 0.0 copy-start.1
  119.7 0.7 copy.34
  120.4 0.3 copy-done.1
  120.7 0.7 copy.35
  (2 shorter events, 0.0 us)
Async XLA Ops:
  1.5 0.7 copy-start.3
  115.6 2.1 %copy-start = (bf16[768,256]{1,0:T(8,128)(2,1)S(1)}, bf16[768,256]{1,0:T(8,128)(2,1)}, u32[]{:S(2)}) copy-start(bf16[768,256]{1,0:T(8,128)(2,1)} %get-tuple-element.16) | copy-start | bytes 1179652
  117.7 2.0 %copy-start.2 = (bf16[256,256]{1,0:T(8,128)(2,1)S(1)}, bf16[256,256]{1,0:T(8,128)(2,1)}, u32[]{:S(2)}) copy-start(bf16[256,256]{1,0:T(8,128)(2,1)} %get-tuple-element.14) | copy-start | bytes 393220
  119.7 1.0 copy-start.1

commit v2 on v1

--- a/solution.py
+++ b/solution.py
@@ -17,6 +17,7 @@
 SEND_AT = 16
 GEO_AT = 88
 DEPTH = 128
+UNROLL = 2
 
 
 def round16(rows):
@@ -78,6 +79,7 @@
     grad_latent,
     out_a,
     out_b,
+    out_few,
     ext,
     gext,
     recv,
@@ -101,7 +103,6 @@
     geo,
     mat,
     mat_t,
-    weight,
     geo_b,
     halo_send,
     halo_recv,
@@ -109,9 +110,13 @@
     part_b,
     got_a,
     got_b,
+    few,
+    few_y,
+    few_x,
     pos_sems,
     halo_sems,
     red_sems,
+    few_sems,
 ):
     slots = 8
     cells = cells_x * cells_y
@@ -263,82 +268,92 @@
     wgt = jnp.where((both > 1.5) & jnp.logical_not(same), 1.0 / (1.0 + dist), 0.0)
     for f, value in enumerate((disp_x, disp_y, dist, wgt)):
         geo[f] = value
-    spread_row = lax.broadcasted_iota(jnp.int32, (DEPTH, 128), 0)
-    spreads = ((spread_row == GEO_AT + 9) | (spread_row == GEO_AT + 10)).astype(F32).astype(BF16)
     row16 = lax.broadcasted_iota(jnp.int32, (16, wide), 0)
+    rest = jnp.zeros((DEPTH - GEO_AT - 16, wide), F32)
 
     def prepare(c, carry):
+        w = geo[3, pl.ds(c, 1)]
+        w_hi = rounded(w)
         tile = jnp.zeros((16, wide), F32)
-        for f in range(4):
+        tile_w = jnp.zeros((16, wide), F32)
+        for f in range(3):
             value = geo[f, pl.ds(c, 1)]
             hi = rounded(value)
-            lo = value - hi
             at = 3 * f
-            if f < 3:
-                tile = jnp.where((row16 == at) | (row16 == at + 2), hi, tile)
-            else:
-                tile = jnp.where(row16 == at, hi, tile)
-            tile = jnp.where(row16 == at + 1, lo, tile)
-        full = jnp.concatenate(
-            [one_hot[:GEO_AT], tile, jnp.zeros((DEPTH - GEO_AT - 16, wide), F32)], axis=0
+            tile = jnp.where((row16 == at) | (row16 == at + 2), hi, tile)
+            tile = jnp.where(row16 == at + 1, value - hi, tile)
+            value = value * w
+            hi = rounded(value)
+            tile_w = jnp.where(row16 == at, hi, tile_w)
+            tile_w = jnp.where(row16 == at + 1, value - hi, tile_w)
+        full = jnp.concatenate([one_hot[:GEO_AT], tile, rest], axis=0)
+        mat[c] = full.T[:pairs].astype(BF16)
+        full_w = jnp.concatenate(
+            [
+                one_hot[:slots] * w_hi,
+                one_hot[slots:SEND_AT] * (w - w_hi),
+                one_hot[SEND_AT:GEO_AT] * w,
+                tile_w,
+                rest,
+            ],
+            axis=0,
         )
-        mat_t[c] = full[:, :pairs].astype(BF16)
-        turned = full.T[:pairs].astype(BF16)
-        mat[c] = turned
-        weight[c] = jnp.dot(turned, spreads, preferred_element_type=F32)
+        mat_t[c] = full_w[:, :pairs].astype(BF16)
         return carry
 
     lax.fori_loop(0, cells, prepare, 0)
 
-    def half_preact(step, c):
-        x, y = lax.div(c, cells_y), lax.rem(c, cells_y)
+    def half_preact(step, x, y):
+        c = x * cells_y + y
         r = recv[step, c] * 0.5
         hi = rounded(r)
         tiles = [hi, r - hi]
         tiles += [ext[step, x + 1 + ox, y + 1 + oy] for ox, oy in OFFSETS]
         b = jnp.concatenate(tiles + [geo_b[...]], axis=0).astype(BF16)
-        return jnp.dot(mat[c], b, preferred_element_type=F32)
-
-    block = slots * slots
-
-    def weights_of(c, o):
-        w = weight[c, o * block : (o + 1) * block]
-        return jnp.concatenate([w] * (width // 128), axis=1).reshape(slots, slots, width)
-
-    def forward_pairs(step):
-        def body(c, carry):
-            q = half_preact(step, c)
-            total = jnp.zeros((slots, width), F32)
-            for o in range(9):
-                part = q[o * block : (o + 1) * block].reshape(slots, slots, width)
-                total = total + jnp.sum(weights_of(c, o) * (part + part * jnp.tanh(part)), axis=0)
-            agg[c] = total
+        return jnp.dot(mat[c], b, preferred_element_type=F32).astype(BF16)
+
+    def inner_cells(body):
+        across = cells_y - 2
+
+        def one(i, carry):
+            body(1 + lax.div(i, across), 1 + lax.rem(i, across))
             return carry
 
-        lax.fori_loop(0, cells, body, 0)
-
-    def backward_pairs(step):
-        gext[...] = jnp.zeros(gext.shape, F32)
-
-        def body(c, carry):
-            x, y = lax.div(c, cells_y), lax.rem(c, cells_y)
-            q = half_preact(step, c)
-            up = (g_agg[c] * 0.5)[None]
-            parts = []
-            for o in range(9):
-                part = q[o * block : (o + 1) * block].reshape(slots, slots, width)
-                t = jnp.tanh(part)
-                d = (weights_of(c, o) * up) * ((1.0 + t) * (1.0 + (part - part * t)))
-                parts.append(d.reshape(block, width).astype(BF16))
-            back = jnp.dot(mat_t[c], jnp.concatenate(parts, axis=0), preferred_element_type=F32)
-            g_recv[c] = back[:slots]
-            for o, (ox, oy) in enumerate(OFFSETS):
-                at = SEND_AT + o * slots
-                gext[x + 1 + ox, y + 1 + oy] += back[at : at + slots]
-            acc_geo[...] += back[GEO_AT : GEO_AT + 16]
+        lax.fori_loop(0, (cells_x - 2) * across, one, 0, unroll=UNROLL)
+
+    def edge_cells(body):
+        def row(i, carry):
+            body(lax.div(i, cells_y) * (cells_x - 1), lax.rem(i, cells_y))
             return carry
 
-        lax.fori_loop(0, cells, body, 0)
+        def column(i, carry):
+            body(1 + lax.div(i, 2), lax.rem(i, 2) * (cells_y - 1))
+            return carry
+
+        lax.fori_loop(0, 2 * cells_y, row, 0, unroll=UNROLL)
+        lax.fori_loop(0, 2 * (cells_x - 2), column, 0, unroll=UNROLL)
+
+    def forward_cell(step, x, y):
+        c = x * cells_y + y
+        q = half_preact(step, x, y)
+        both_parts = jnp.dot(
+            mat_t[c, :SEND_AT], q + q * jnp.tanh(q), preferred_element_type=F32
+        )
+        agg[c] = both_parts[:slots] + both_parts[slots:]
+
+    def backward_cell(step, x, y):
+        c = x * cells_y + y
+        q = half_preact(step, x, y).reshape(-1, 2 * slots, width)
+        up = g_agg[c] * 0.5
+        up = jnp.concatenate([up, up], axis=0).astype(BF16)[None]
+        t = jnp.tanh(q)
+        d = up * ((1.0 + t) * (1.0 + (q - q * t)))
+        back = jnp.dot(mat_t[c], d.reshape(pairs, width), preferred_element_type=F32)
+        g_recv[c] = back[:slots] + back[slots:SEND_AT]
+        for o, (ox, oy) in enumerate(OFFSETS):
+            at = SEND_AT + o * slots
+            gext[x + 1 + ox, y + 1 + oy] += back[at : at + slots]
+        acc_geo[...] += back[GEO_AT : GEO_AT + 16]
 
     gain = gain_ref[...]
 
@@ -360,11 +375,12 @@
         rstd[step] = jnp.broadcast_to(scale, rstd.shape[1:])
         return (hs[step].astype(F32) + normed * gain).astype(BF16)
 
-    arrive(0)
-    forward_pairs(0)
-    project(1, node_forward(0))
-    arrive(1)
-    forward_pairs(1)
+    for step in range(STEPS):
+        inner_cells(partial(forward_cell, step))
+        arrive(step)
+        edge_cells(partial(forward_cell, step))
+        if step == 0:
+            project(1, node_forward(0))
     latent_out[...] = node_forward(1)
 
     def spread_out(part, got, share, sem):
@@ -405,6 +421,18 @@
         size = result.at[pl.ds(0, (n - 1) * share)]
         wait_all(size, red_sems.at[1, sem + 1])
         wait_all(size, red_sems.at[0, sem + 1])
+
+    def sum_few_start(stage, axis, size, here, got):
+        for k in range(1, size):
+            pltpu.make_async_remote_copy(
+                few.at[stage], got.at[k - 1], few_sems.at[0, stage], few_sems.at[1, stage],
+                device_id={axis: lax.rem(here + k, size)}, device_id_type=MESH,
+            ).start()
+
+    def sum_few_end(stage, got):
+        wait_all(got, few_sems.at[1, stage])
+        wait_all(got, few_sems.at[0, stage])
+        few[stage + 1] = few[stage] + jnp.sum(got[...], axis=0)
 
     share_a = got_a.shape[1]
     share_b = got_b.shape[1]
@@ -452,7 +480,8 @@
                 )
             spread_out(part_a, got_a, share_a, 0)
         g_agg[...] = rounded(mm_t(d_msg, w_msg[...])).reshape(cells, slots, width)
-        backward_pairs(step)
+        gext[...] = jnp.zeros(gext.shape, F32)
+        edge_cells(partial(backward_cell, step))
 
         def taken(dx, dy):
             return [
@@ -462,11 +491,18 @@
             ]
 
         start_halo(STEPS + step, taken)
+        if last:
+            gather_in(part_a, got_a, share_a, out_a, 0)
+        inner_cells(partial(backward_cell, step))
+        if last:
+            sums = acc_geo[...]
+            tail = [sums[3 * f : 3 * f + 1] + sums[3 * f + 1 : 3 * f + 2] for f in range(3)]
+            tail += [acc_small[0:1], jnp.zeros((4, width), F32)]
+            few[0] = jnp.concatenate(tail, axis=0)
+            sum_few_start(0, "gy", ngy, gy, few_y)
         d_recv = g_recv[...].reshape(cells * slots, width)
         put(4, outer(hs[step], d_recv))
         d_h = flow32 + rounded(mm_t(d_hid, w_nh[...])) + rounded(mm_t(d_recv, w_recv[...]))
-        if last:
-            gather_in(part_a, got_a, share_a, out_a, 0)
         end_halo(STEPS + step)
         for d, (dx, dy) in enumerate(SIDES):
             at, rows_d = segs[d]
@@ -487,16 +523,18 @@
         ).astype(BF16)
         put(5, outer(hs[step], d_send))
         if last:
-            sums = acc_geo[...]
-            tail = [sums[3 * f : 3 * f + 1] + sums[3 * f + 1 : 3 * f + 2] for f in range(3)]
-            tail.append(acc_small[0:1])
-            rest = part_b.shape[0] - 2 * width
-            tail.append(jnp.zeros((rest - 4, width), F32))
-            part_b[pl.ds(2 * width, rest)] = jnp.concatenate(tail, axis=0).astype(BF16)
+            if part_b.shape[0] > 2 * width:
+                part_b[pl.ds(2 * width, part_b.shape[0] - 2 * width)] = jnp.zeros(
+                    (part_b.shape[0] - 2 * width, width), BF16
+                )
             spread_out(part_b, got_b, share_b, 2)
+            sum_few_end(0, few_y)
+            sum_few_start(1, "gx", ngx, gx, few_x)
         flow = (d_h + rounded(mm_t(d_send, w_send[...]))).astype(BF16)
     grad_latent[...] = flow
     gather_in(part_b, got_b, share_b, out_b, 2)
+    sum_few_end(1, few_x)
+    out_few[...] = few[2]
     gathered(share_a, out_a, 0)
     gathered(share_b, out_b, 2)
 
@@ -536,7 +574,7 @@
     wide = -(-pairs // 128) * 128
     _, halo_rows = segments(cells_x, cells_y, slots)
     share_a = round16(-(-4 * width // n))
-    share_b = round16(-(-(2 * width + 16) // n))
+    share_b = round16(-(-2 * width // n))
     vmem = pltpu.VMEM
     scratch = [
         vmem((STEPS, cells_x + 2, cells_y + 2, slots, width), F32),
@@ -562,7 +600,6 @@
         vmem((4, cells, wide), F32),
         vmem((cells, pairs, DEPTH), BF16),
         vmem((cells, DEPTH, pairs), BF16),
-        vmem((cells, pairs, 128), F32),
         vmem((DEPTH - GEO_AT, width), F32),
         vmem((2 * STEPS, halo_rows, width), BF16),
         vmem((2 * STEPS, halo_rows, width), BF16),
@@ -570,21 +607,26 @@
         vmem((n * share_b, width), BF16),
         vmem((n - 1, share_a, width), BF16),
         vmem((n - 1, share_b, width), BF16),
+        vmem((3, 8, width), F32),
+        vmem((ngy - 1, 8, width), F32),
+        vmem((ngx - 1, 8, width), F32),
         pltpu.SemaphoreType.DMA((2,)),
         pltpu.SemaphoreType.DMA((2, 2 * STEPS)),
         pltpu.SemaphoreType.DMA((2, 4)),
+        pltpu.SemaphoreType.DMA((2, 2)),
     ]
     spec = pl.BlockSpec(memory_space=pltpu.VMEM)
-    new, flow, sums_a, sums_b = pl.pallas_call(
+    new, flow, sums_a, sums_b, sums_few = pl.pallas_call(
         partial(kernel, ngx, ngy, cells_x, cells_y),
         out_shape=[
             jax.ShapeDtypeStruct((rows, width), BF16),
             jax.ShapeDtypeStruct((rows, width), BF16),
             jax.ShapeDtypeStruct((n * share_a, width), BF16),
             jax.ShapeDtypeStruct((n * share_b, width), BF16),
+            jax.ShapeDtypeStruct((8, width), F32),
         ],
         in_specs=[spec] * 11,
-        out_specs=[spec] * 4,
+        out_specs=[spec] * 5,
         scratch_shapes=scratch,
         compiler_params=pltpu.CompilerParams(
             collective_id=0, has_side_effects=True, vmem_limit_bytes=56 * 2**20
@@ -616,8 +658,8 @@
         piece(sums_a, width, width),
         piece(sums_a, 2 * width, width),
         piece(sums_a, 3 * width, width),
-        piece(sums_b, 2 * width, 3),
-        piece(sums_b, 2 * width + 3, 1).reshape(width),
+        sums_few[:3],
+        sums_few[3],
     )
 
 

time: 124 us -> 104 us (0.84); the launches traced: 121 us -> 104 us
  Pallas kernels: 113 us -> 95.1 us
    pallas_call x1, Pallas kernels: 113 us -> 95.1 us  [per_device(): pl.pallas_call(partial(kernel, ngx, ngy, cells_x, cells_y), out_shape=[ja...]
    convert_element_type x3 -> x2, other arithmetic: 3.54 us -> 2.94 us  [piece(): return sums[at:at + size].astype(F32)]
where the time goes in v2:
time: 104 us
  Pallas kernels  95.1 us (91%)
  local copies, waits for them, and re-layouts  4.35 us (4%)
  other arithmetic  3.71 us (4%)
    pallas_call x1, Pallas kernels, per_device(): pl.pallas_call(partial(kernel, ngx, ngy, cells_x, cells_y), out_shape=[ja...  95.1 us
    convert_element_type x2, other arithmetic, piece(): return sums[at:at + size].astype(F32)  2.94 us
    unnamed x12, local copies, waits for them, and re-layouts  2.29 us

profile of v2, /device:TPU:0, one launch (start us, length us, event | category | flops | bytes accessed | tf_op | source)
XLA Modules:
  0.0 103.9 jit_solution(11368282735399978767)
XLA Ops:
  0.6 0.8 fusion.3
  1.5 0.0 copy-start.4
  1.5 0.7 copy-done.4
  2.2 0.1 fusion
  2.2 0.1 pad.3.clone
  2.3 0.7 maximum_maximum_fusion.cell_ref
  3.0 95.1 %evolver.1 = (bf16[256,256]{1,0:T(8,128)(2,1)}, bf16[256,256]{1,0:T(8,128)(2,1)}, bf16[1024,256]{1,0:T(8,128)(2,1)}, bf16[512,256]{1,0:T(8,128)(2,1)}, f32[8,256]{1,0:T(8,128)}) custom-call(bf16[256,256]{1,0:T(8,128)(2,1)} %bitcast.16, f32[4,8,128]{2,1,0:T(8,128)} %maximum_maximum_fusion.cell_ref, bf16[256,256]{1,0:T(8,128)(2,1)} %bitcast.17, ...), custom_call_target="tpu_custom_call" | custom-call | tf_op jit(solution)/shard_map/evolver/pallas_call | solution.py:619
  98.1 0.0 copy-start
  98.2 2.1 %slice_convert_fusion = (f32[256,256]{1,0:T(8,128)}, f32[256,256]{1,0:T(8,128)}, f32[256,256]{1,0:T(8,128)}, f32[256,256]{1,0:T(8,128)}) fusion(bf16[1024,256]{1,0:T(8,128)(2,1)} %get-tuple-element.18), kind=kLoop, calls=%fused_computation | loop fusion | flops 262144 | bytes 1572864 | tf_op jit(solution)/shard_map/convert_element_type | solution.py:650
  100.3 0.0 copy-done
  100.3 0.0 copy-start.3
  100.3 0.0 copy-start.2
  100.3 0.8 slice_convert_fusion.4
  101.1 0.0 copy-done.3
  101.1 0.6 slice.38
  101.7 0.6 slice.39
  102.3 0.0 copy-done.2
  102.3 0.0 copy-start.1
  102.3 0.7 copy.34
  102.9 0.3 copy-done.1
  103.2 0.7 copy.35
  (2 shorter events, 0.0 us)
Async XLA Ops:
  1.5 0.7 copy-start.4
  98.1 2.1 %copy-start = (bf16[512,256]{1,0:T(8,128)(2,1)S(1)}, bf16[512,256]{1,0:T(8,128)(2,1)}, u32[]{:S(2)}) copy-start(bf16[512,256]{1,0:T(8,128)(2,1)} %get-tuple-element.17) | copy-start | bytes 786436
  100.3 0.8 copy-start.3
  100.3 2.0 %copy-start.2 = (bf16[256,256]{1,0:T(8,128)(2,1)S(1)}, bf16[256,256]{1,0:T(8,128)(2,1)}, u32[]{:S(2)}) copy-start(bf16[256,256]{1,0:T(8,128)(2,1)} %get-tuple-element.15) | copy-start | bytes 393220
  102.3 1.0 copy-start.1

commit v3 on v2

--- a/solution.py
+++ b/solution.py
@@ -17,7 +17,7 @@
 SEND_AT = 16
 GEO_AT = 88
 DEPTH = 128
-UNROLL = 2
+UNROLL = 4
 
 
 def round16(rows):
@@ -301,7 +301,7 @@
         mat_t[c] = full_w[:, :pairs].astype(BF16)
         return carry
 
-    lax.fori_loop(0, cells, prepare, 0)
+    lax.fori_loop(0, cells, prepare, 0, unroll=UNROLL)
 
     def half_preact(step, x, y):
         c = x * cells_y + y
@@ -310,7 +310,7 @@
         tiles = [hi, r - hi]
         tiles += [ext[step, x + 1 + ox, y + 1 + oy] for ox, oy in OFFSETS]
         b = jnp.concatenate(tiles + [geo_b[...]], axis=0).astype(BF16)
-        return jnp.dot(mat[c], b, preferred_element_type=F32).astype(BF16)
+        return jnp.dot(mat[c], b, preferred_element_type=F32)
 
     def inner_cells(body):
         across = cells_y - 2
@@ -337,13 +337,13 @@
         c = x * cells_y + y
         q = half_preact(step, x, y)
         both_parts = jnp.dot(
-            mat_t[c, :SEND_AT], q + q * jnp.tanh(q), preferred_element_type=F32
+            mat_t[c, :SEND_AT], (q + q * jnp.tanh(q)).astype(BF16), preferred_element_type=F32
         )
         agg[c] = both_parts[:slots] + both_parts[slots:]
 
     def backward_cell(step, x, y):
         c = x * cells_y + y
-        q = half_preact(step, x, y).reshape(-1, 2 * slots, width)
+        q = half_preact(step, x, y).astype(BF16).reshape(-1, 2 * slots, width)
         up = g_agg[c] * 0.5
         up = jnp.concatenate([up, up], axis=0).astype(BF16)[None]
         t = jnp.tanh(q)

time: 104 us -> 97.1 us (0.934)
  Pallas kernels: 95.1 us -> 88 us
    pallas_call x1, Pallas kernels: 95.1 us -> 88 us  [per_device(): pl.pallas_call(partial(kernel, ngx, ngy, cells_x, cells_y), out_shape=[ja...]
where the time goes in v3:
time: 97.1 us; the launch traced here: 96.7 us
  Pallas kernels  88 us (91%)
  local copies, waits for them, and re-layouts  4.35 us (4%)
  other arithmetic  3.71 us (4%)
    pallas_call x1, Pallas kernels, per_device(): pl.pallas_call(partial(kernel, ngx, ngy, cells_x, cells_y), out_shape=[ja...  88 us
    convert_element_type x2, other arithmetic, piece(): return sums[at:at + size].astype(F32)  2.94 us
    unnamed x12, local copies, waits for them, and re-layouts  2.29 us

profile of v3, /device:TPU:0, one launch (start us, length us, event | category | flops | bytes accessed | tf_op | source)
XLA Modules:
  0.0 96.7 jit_solution(12431270703631482892)
XLA Ops:
  0.6 0.8 fusion.3
  1.5 0.0 copy-start.4
  1.5 0.7 copy-done.4
  2.2 0.1 fusion
  2.2 0.1 pad.3.clone
  2.3 0.7 maximum_maximum_fusion.cell_ref
  3.0 88.0 %evolver.1 = (bf16[256,256]{1,0:T(8,128)(2,1)}, bf16[256,256]{1,0:T(8,128)(2,1)}, bf16[1024,256]{1,0:T(8,128)(2,1)}, bf16[512,256]{1,0:T(8,128)(2,1)}, f32[8,256]{1,0:T(8,128)}) custom-call(bf16[256,256]{1,0:T(8,128)(2,1)} %bitcast.16, f32[4,8,128]{2,1,0:T(8,128)} %maximum_maximum_fusion.cell_ref, bf16[256,256]{1,0:T(8,128)(2,1)} %bitcast.17, ...), custom_call_target="tpu_custom_call" | custom-call | tf_op jit(solution)/shard_map/evolver/pallas_call | solution.py:619
  91.0 0.0 copy-start
  91.0 2.1 %slice_convert_fusion = (f32[256,256]{1,0:T(8,128)}, f32[256,256]{1,0:T(8,128)}, f32[256,256]{1,0:T(8,128)}, f32[256,256]{1,0:T(8,128)}) fusion(bf16[1024,256]{1,0:T(8,128)(2,1)} %get-tuple-element.18), kind=kLoop, calls=%fused_computation | loop fusion | flops 262144 | bytes 1572864 | tf_op jit(solution)/shard_map/convert_element_type | solution.py:650
  93.1 0.0 copy-done
  93.1 0.0 copy-start.3
  93.1 0.0 copy-start.2
  93.1 0.8 slice_convert_fusion.4
  94.0 0.0 copy-done.3
  94.0 0.6 slice.38
  94.6 0.6 slice.39
  95.1 0.0 copy-done.2
  95.1 0.0 copy-start.1
  95.1 0.7 copy.34
  95.8 0.3 copy-done.1
  96.1 0.7 copy.35
  (2 shorter events, 0.0 us)
Async XLA Ops:
  1.5 0.7 copy-start.4
  91.0 2.1 %copy-start = (bf16[512,256]{1,0:T(8,128)(2,1)S(1)}, bf16[512,256]{1,0:T(8,128)(2,1)}, u32[]{:S(2)}) copy-start(bf16[512,256]{1,0:T(8,128)(2,1)} %get-tuple-element.17) | copy-start | bytes 786436
  93.1 0.8 copy-start.3
  93.1 2.0 %copy-start.2 = (bf16[256,256]{1,0:T(8,128)(2,1)S(1)}, bf16[256,256]{1,0:T(8,128)(2,1)}, u32[]{:S(2)}) copy-start(bf16[256,256]{1,0:T(8,128)(2,1)} %get-tuple-element.15) | copy-start | bytes 393220
  95.1 1.0 copy-start.1
